TPU v7x, 256 devices: a whole 4x4x8 slice. The times are simulated.
256 devices in a mesh: grp: 32 (over z, x_lo, core), tp: 8 (over y, x_hi).
Axes of the slice: x: 4 (x_hi: 2, x_lo: 2; x = x_hi * 2 + x_lo), y: 4, z: 8, core: 2. Of those that a mesh axis runs over, the one named last changes fastest.
Arguments:
- queries: bfloat16 [8192, 4096], P('grp', 'tp'), may hold values from -60 to 60
- key_rows: bfloat16 [8192, 1024], P('grp', 'tp'), may hold values from -6 to 6
- value_rows: bfloat16 [8192, 1024], P('grp', 'tp'), may hold values from -6 to 6
- out_weight: bfloat16 [4096, 8192], P('tp'), may hold values from -1.5 to 1.5
- block_order: int32 [32], replicated, may hold values from 0 to 31, each once
- page_owner: int32 [512, 1], replicated, may hold values from 0 to 31, as said below
Outputs:
- attention_out: bfloat16 [8192, 8192], P('grp', 'tp')
- page_cache: bfloat16 [2048, 16, 2048], P('grp', None, 'tp')
Inputs may be any that keep to these rules, and one draw needn't show every extreme that they name: `page_owner`: the 16 pages of one device name each owner at most 2 times; one owner is named exactly 2 times by every device.
All inputs are finite; a program needn't handle non-finite values.
Results may differ from a plain program's by a relative error of at most 0.017.
Values may be sent and summed in bfloat16 or wider, within the bound.
A program may use at most 64 MiB of HBM per device.

v0:
```python
import math

import jax
import jax.numpy as jnp
from jax import lax
from jax.sharding import PartitionSpec as P

HEAD_DIM = 128
QPK = 4
PAGE = 16
MOST = 2


masked_score = -1e30


def softmax_update(running, query_tile, query_pos, key_tile, value_tile, key_pos, score_scale):
    row_peak, row_total, row_accum = running
    scores = (
        jnp.einsum("chd,kd->hck", query_tile, key_tile, preferred_element_type=jnp.float32)
        * score_scale
    )
    allowed = key_pos[None, None, :] <= query_pos[None, :, None]
    scores = jnp.where(allowed, scores, masked_score)
    new_peak = jnp.maximum(row_peak, jnp.max(scores, axis=-1))
    factor = jnp.exp(row_peak - new_peak)
    exponent = jnp.where(allowed, jnp.exp(scores - new_peak[..., None]), 0.0)
    row_total = row_total * factor + jnp.sum(exponent, axis=-1)
    weights = exponent.astype(jnp.bfloat16)
    row_accum = row_accum * factor[..., None] + jnp.einsum(
        "hck,kd->hcd", weights, value_tile, preferred_element_type=jnp.float32
    )
    return (new_peak, row_total, row_accum)


def empty_state(heads_here, row_count, head_dim):
    return (
        jnp.full((heads_here, row_count), masked_score, jnp.float32),
        jnp.zeros((heads_here, row_count), jnp.float32),
        jnp.zeros((heads_here, row_count, head_dim), jnp.float32),
    )


def finish_rows(running):
    row_peak, row_total, row_accum = running
    return (row_accum / row_total[..., None]).astype(jnp.bfloat16)


def on_device(queries, key_rows, value_rows, out_weight, block_order, page_owner):
    rows_dev, head_dim = key_rows.shape
    groups = lax.axis_size("grp")
    own_index = lax.axis_index("grp")
    score_scale = HEAD_DIM ** (-0.5)
    group_ids = jnp.arange(groups, dtype=jnp.int32)
    local_queries = queries.reshape(rows_dev, QPK, head_dim)
    query_pos = block_order[own_index] * rows_dev + jnp.arange(rows_dev, dtype=jnp.int32)
    top_query = jnp.max(query_pos)
    running = empty_state(QPK, rows_dev, head_dim)
    key_piece = lax.all_gather(key_rows, "grp", axis=0, tiled=True)
    value_piece = lax.all_gather(value_rows, "grp", axis=0, tiled=True)
    piece_rows = key_piece.shape[0]
    tile_width = math.gcd(piece_rows, 512)
    steps_n = piece_rows // tile_width
    key_blocks = key_piece.reshape(steps_n, tile_width, head_dim)
    value_blocks = value_piece.reshape(steps_n, tile_width, head_dim)

    def one_step(state_now, inputs):
        key_tile, value_tile, offset = inputs
        global_row = offset + jnp.arange(tile_width, dtype=jnp.int32)
        holder = global_row // rows_dev
        block_place = jnp.sum(
            jnp.where(holder[:, None] == group_ids[None, :], block_order[None, :], 0), axis=1
        )
        key_pos = block_place * rows_dev + global_row % rows_dev

        def compute(state_in):
            return softmax_update(
                state_in, local_queries, query_pos, key_tile, value_tile, key_pos, score_scale
            )

        def keep(state_in):
            return state_in

        state_now = lax.cond(jnp.min(key_pos) > top_query, keep, compute, state_now)
        return (state_now, None)

    offsets = jnp.arange(steps_n, dtype=jnp.int32) * tile_width
    running, unused = lax.scan(one_step, running, (key_blocks, value_blocks, offsets))
    attended = jnp.transpose(finish_rows(running), (1, 0, 2)).reshape(rows_dev, QPK * head_dim)
    partial_term = jnp.dot(attended, out_weight, preferred_element_type=jnp.float32)
    attention_out = lax.psum_scatter(
        partial_term.astype(jnp.bfloat16), "tp", scatter_dimension=1, tiled=True
    )
    owners = page_owner[:, 0].reshape(groups, -1)
    own_owners = lax.dynamic_slice_in_dim(owners, own_index, 1, 0)[0]
    pages_dev = own_owners.shape[0]
    page_ids = jnp.arange(pages_dev, dtype=jnp.int32)
    earlier = page_ids[None, :] < page_ids[:, None]
    same_owner = own_owners[None, :] == own_owners[:, None]
    page_rank = jnp.sum(jnp.where(earlier & same_owner, 1, 0), axis=1)
    target_row = own_owners * MOST + page_rank
    slot_ids = jnp.arange(groups * MOST, dtype=jnp.int32)
    picker = (slot_ids[:, None] == target_row[None, :]).astype(jnp.bfloat16)
    page_rows = jnp.concatenate([key_rows, value_rows], axis=1).reshape(
        pages_dev, PAGE * 2 * head_dim
    )
    outgoing = jnp.dot(picker, page_rows, preferred_element_type=jnp.float32).astype(jnp.bfloat16)
    outgoing = outgoing.reshape(groups, MOST, PAGE * 2 * head_dim)
    arrived = lax.all_to_all(outgoing, "grp", split_axis=0, concat_axis=0, tiled=True)
    page_counts = jnp.sum(jnp.where(owners == own_index, 1, 0), axis=1)
    first_slot = jnp.cumsum(page_counts) - page_counts
    within = jnp.arange(MOST, dtype=jnp.int32)[None, :]
    slot_index = jnp.where(within < page_counts[:, None], first_slot[:, None] + within, -1).reshape(
        groups * MOST
    )
    placement = (slot_ids[:, None] == slot_index[None, :]).astype(jnp.bfloat16)
    page_cache = jnp.dot(
        placement,
        arrived.reshape(groups * MOST, PAGE * 2 * head_dim),
        preferred_element_type=jnp.float32,
    ).astype(jnp.bfloat16)
    page_cache = page_cache.reshape(groups * MOST, PAGE, 2 * head_dim)
    return (attention_out, page_cache)


def solution(mesh):
    placed = (P("grp", "tp"), P("grp", "tp"), P("grp", "tp"), P("tp", None), P(), P())
    return jax.shard_map(
        on_device,
        mesh=mesh,
        in_specs=placed,
        out_specs=(P("grp", "tp"), P("grp", None, "tp")),
        check_vma=False,
    )
```

profile of v0, /device:TPU:8, one launch (start us, length us, event | category | flops | bytes accessed | tf_op | source)
XLA Modules:
  0.0 388.6 jit_solution(1013459658069902573)
XLA Ops:
  8.7 1.2 dynamic_slice.32
  11.2 1.1 copy.16
  12.5 64.9 %all-gather.3.cloned.1.call-done = bf16[8192,128]{1,0:T(8,128)(2,1)} async-done(((bf16[256,128]{1,0:T(8,128)(2,1)}), bf16[8192,128]{1,0:T(8,128)(2,1)}) %all-gather.3.cloned.1.call-update) | async-done | bytes 2097168 | tf_op jit(solution)/shard_map/all_gather | solution.py:59
  77.5 66.3 %all-gather.5.cloned.1.call-done = bf16[8192,128]{1,0:T(8,128)(2,1)} async-done(((bf16[256,128]{1,0:T(8,128)(2,1)}), bf16[8192,128]{1,0:T(8,128)(2,1)}) %all-gather.5.cloned.1.call-update) | async-done | bytes 2097168 | tf_op jit(solution)/shard_map/all_gather | solution.py:60
  143.8 98.3 %while.17 = (s32[]{:T(128)}, f32[4,256]{1,0:T(4,128)S(1)}, f32[4,256]{1,0:T(4,128)S(1)}, f32[4,256,128]{2,1,0:T(8,128)S(1)}, s32[16]{0:T(128)S(1)}, /*index=5*/s...) while((s32[]{:T(128)}, f32[4,256]{1,0:T(4,128)S(1)}, ...), condition=%wide.region_8.9_spmd.clone, body=%wide.region_1.8_spmd.clone.sunk | while | flops 275711232 | bytes 8471967 | solution.py:88
  145.0 0.7 select_reduce_fusion.4
  145.8 1.3 fusion.39
  148.4 3.9 %conditional.3 = (f32[4,256]{1,0:T(4,128)S(1)}, f32[4,256]{1,0:T(4,128)S(1)}, f32[4,256,128]{2,1,0:T(8,128)S(1)}) conditional(s32[]{:T(128)} %convert_element_type.37, (s32[512]{0:T(512)S(1)}, s32[]{:T(128)}, bf16[16,512,128]{2,1,0:T(8,128)(2,1)}, s32[]{:T(128)}, bf16[256,4,128]{2,0,1:T(8,128)(2,1)S(1)}, /*index=5*/f32[4,256]{1,0:T(4,128)S(1)}, ...), branch_computations={%region_4.6_spmd, %region_7.7_spmd} | conditional | flops 275646720 | bytes 8452124 | solution.py:84
  148.6 1.4 fusion.4
  150.6 1.8 convolution_add_fusion
  154.4 1.3 fusion.39
  159.1 1.3 fusion.39
  163.7 1.3 fusion.39
  168.4 1.3 fusion.39
  171.1 3.9 %conditional.3 = (f32[4,256]{1,0:T(4,128)S(1)}, f32[4,256]{1,0:T(4,128)S(1)}, f32[4,256,128]{2,1,0:T(8,128)S(1)}) conditional(s32[]{:T(128)} %convert_element_type.37, (s32[512]{0:T(512)S(1)}, s32[]{:T(128)}, bf16[16,512,128]{2,1,0:T(8,128)(2,1)}, s32[]{:T(128)}, bf16[256,4,128]{2,0,1:T(8,128)(2,1)S(1)}, /*index=5*/f32[4,256]{1,0:T(4,128)S(1)}, ...), branch_computations={%region_4.6_spmd, %region_7.7_spmd} | conditional | flops 275646720 | bytes 8452124 | solution.py:84
  171.2 1.4 fusion.4
  173.2 1.8 convolution_add_fusion
  176.3 0.7 select_reduce_fusion.4
  177.0 1.3 fusion.39
  180.9 0.7 select_reduce_fusion.4
  181.7 1.3 fusion.39
  184.3 3.9 %conditional.3 = (f32[4,256]{1,0:T(4,128)S(1)}, f32[4,256]{1,0:T(4,128)S(1)}, f32[4,256,128]{2,1,0:T(8,128)S(1)}) conditional(s32[]{:T(128)} %convert_element_type.37, (s32[512]{0:T(512)S(1)}, s32[]{:T(128)}, bf16[16,512,128]{2,1,0:T(8,128)(2,1)}, s32[]{:T(128)}, bf16[256,4,128]{2,0,1:T(8,128)(2,1)S(1)}, /*index=5*/f32[4,256]{1,0:T(4,128)S(1)}, ...), branch_computations={%region_4.6_spmd, %region_7.7_spmd} | conditional | flops 275646720 | bytes 8452124 | solution.py:84
  184.5 1.4 fusion.4
  186.5 1.8 convolution_add_fusion
  190.3 1.3 fusion.39
  194.9 1.3 fusion.39
  199.6 1.3 fusion.39
  204.3 1.3 fusion.39
  207.0 3.9 %conditional.3 = (f32[4,256]{1,0:T(4,128)S(1)}, f32[4,256]{1,0:T(4,128)S(1)}, f32[4,256,128]{2,1,0:T(8,128)S(1)}) conditional(s32[]{:T(128)} %convert_element_type.37, (s32[512]{0:T(512)S(1)}, s32[]{:T(128)}, bf16[16,512,128]{2,1,0:T(8,128)(2,1)}, s32[]{:T(128)}, bf16[256,4,128]{2,0,1:T(8,128)(2,1)S(1)}, /*index=5*/f32[4,256]{1,0:T(4,128)S(1)}, ...), branch_computations={%region_4.6_spmd, %region_7.7_spmd} | conditional | flops 275646720 | bytes 8452124 | solution.py:84
  207.1 1.4 fusion.4
  209.1 1.8 convolution_add_fusion
  212.9 1.3 fusion.39
  217.6 1.3 fusion.39
  222.3 1.3 fusion.39
  224.9 3.9 %conditional.3 = (f32[4,256]{1,0:T(4,128)S(1)}, f32[4,256]{1,0:T(4,128)S(1)}, f32[4,256,128]{2,1,0:T(8,128)S(1)}) conditional(s32[]{:T(128)} %convert_element_type.37, (s32[512]{0:T(512)S(1)}, s32[]{:T(128)}, bf16[16,512,128]{2,1,0:T(8,128)(2,1)}, s32[]{:T(128)}, bf16[256,4,128]{2,0,1:T(8,128)(2,1)S(1)}, /*index=5*/f32[4,256]{1,0:T(4,128)S(1)}, ...), branch_computations={%region_4.6_spmd, %region_7.7_spmd} | conditional | flops 275646720 | bytes 8452124 | solution.py:84
  225.1 1.4 fusion.4
  227.0 1.8 convolution_add_fusion
  230.8 1.3 fusion.39
  235.5 1.3 fusion.39
  238.2 3.9 %conditional.3 = (f32[4,256]{1,0:T(4,128)S(1)}, f32[4,256]{1,0:T(4,128)S(1)}, f32[4,256,128]{2,1,0:T(8,128)S(1)}) conditional(s32[]{:T(128)} %convert_element_type.37, (s32[512]{0:T(512)S(1)}, s32[]{:T(128)}, bf16[16,512,128]{2,1,0:T(8,128)(2,1)}, s32[]{:T(128)}, bf16[256,4,128]{2,0,1:T(8,128)(2,1)S(1)}, /*index=5*/f32[4,256]{1,0:T(4,128)S(1)}, ...), branch_computations={%region_4.6_spmd, %region_7.7_spmd} | conditional | flops 275646720 | bytes 8452124 | solution.py:84
  238.3 1.4 fusion.4
  240.3 1.8 convolution_add_fusion
  242.4 7.7 %convolution_convert_fusion = bf16[256,8192]{1,0:T(8,128)(2,1)} fusion(bf16[256,512]{0,1:T(8,128)(2,1)S(1)} %bitcast.49, bf16[512,8192]{1,0:T(8,128)(2,1)} %param.13), kind=kOutput, calls=%fused_computation.39 | convolution fusion | flops 2149580800 | bytes 12845056 | tf_op jit(solution)/shard_map/dot_general | solution.py:90
  252.1 1.1 reshape.153
  253.2 44.6 %all-to-all-start = ((bf16[32,2,4096]{2,1,0:T(2,128)(2,1)}), bf16[32,2,4096]{2,1,0:T(2,128)(2,1)S(1)}, u32[]{:S(2)}, u32[]{:S(2)}) async-start(bf16[32,2,4096]{2,1,0:T(2,128)(2,1)} %reshape.153), calls=%async_computation.1 | async-start | bytes 1048576 | tf_op jit(solution)/shard_map/all_to_all | solution.py:109
  298.4 17.5 %all-to-all-done = bf16[32,2,4096]{2,1,0:T(2,128)(2,1)S(1)} async-done(((bf16[32,2,4096]{2,1,0:T(2,128)(2,1)}), bf16[32,2,4096]{2,1,0:T(2,128)(2,1)S(1)}, u32[]{:S(2)}, u32[]{:S(2)}) %all-to-all-start) | async-done | bytes 524320 | tf_op jit(solution)/shard_map/all_to_all | solution.py:109
  316.3 0.9 copy.21
  317.2 64.9 %reduce-scatter.2.cloned.1.call-done = bf16[256,1024]{1,0:T(8,128)(2,1)} async-done(((bf16[256,8192]{1,0:T(8,128)(2,1)}), bf16[256,1024]{1,0:T(8,128)(2,1)}) %reduce-scatter.2.cloned.1.call-update) | async-done | bytes 524304 | tf_op jit(solution)/shard_map/reduce_scatter | solution.py:91
  (165 shorter events, 39.6 us)
Async XLA Ops:
  7.2 70.3 %all-gather.3.cloned.1.call-start = ((), (), s32[]{:S(2)}) async-start(), calls=%async_computation.2 | async-start | bytes 2162688 | tf_op jit(solution)/shard_map/all_gather | solution.py:59
  7.9 135.8 %all-gather.5.cloned.1.call-start = ((), (), s32[]{:S(2)}) async-start(), calls=%async_computation.3 | async-start | bytes 2162688 | tf_op jit(solution)/shard_map/all_gather | solution.py:60
  8.6 373.5 %reduce-scatter.2.cloned.1.call-start = ((), (), s32[]{:S(2)}) async-start(), calls=%async_computation.4 | async-start | bytes 4718592 | tf_op jit(solution)/shard_map/reduce_scatter | solution.py:91
  250.1 0.7 copy-start.2
  250.1 1.4 copy-start
  250.1 1.4 copy-start.1
  253.2 62.6 %all-to-all-start = ((bf16[32,2,4096]{2,1,0:T(2,128)(2,1)}), bf16[32,2,4096]{2,1,0:T(2,128)(2,1)S(1)}, u32[]{:S(2)}, u32[]{:S(2)}) async-start(bf16[32,2,4096]{2,1,0:T(2,128)(2,1)} %reshape.153), calls=%async_computation.1 | async-start | bytes 1048576 | tf_op jit(solution)/shard_map/all_to_all | solution.py:109
Sparse Core Ops, SparseCore 0:
  9.9 67.5 all-gather.2
  79.3 64.3 all-gather.4
  250.2 131.8 reduce-scatter.1
where the time goes:
time: 390 us; the launch traced here: 389 us
  waiting for transfers between devices  215 us (55%)
  other arithmetic  49.1 us (13%)
  starting transfers between devices  44.7 us (11%)
  matrix products  27.2 us (7%)
  loops' own time  22.2 us (6%)
  local copies, waits for them, and re-layouts  16 us (4%)
  between operations  14.5 us (4%)
    all_gather x1, waiting for transfers between devices, on_device(): value_piece = lax.all_gather(value_rows, 'grp', axis=0, tiled=True)  66.3 us
    all_gather x1, waiting for transfers between devices, on_device(): key_piece = lax.all_gather(key_rows, 'grp', axis=0, tiled=True)  64.9 us
    reduce_scatter x1, waiting for transfers between devices, on_device(): lax.psum_scatter(partial_term.astype(jnp.bfloat16), 'tp', scatter_dimensi...  64.9 us
    all_to_all x1, starting transfers between devices, on_device(): lax.all_to_all(outgoing, 'grp', split_axis=0, concat_axis=0, tiled=True)  44.6 us
    another operation x1, loops' own time, on_device(): lax.scan(one_step, running, (key_blocks, value_blocks, offsets))  21.6 us
    reduce_min x16, other arithmetic, one_step(): state_now = lax.cond(jnp.min(key_pos) > top_query, keep, compute, state_now)  21.2 us
    all_to_all x1, waiting for transfers between devices, on_device(): lax.all_to_all(outgoing, 'grp', split_axis=0, concat_axis=0, tiled=True)  17.5 us
    reduce_sum x16, other arithmetic, one_step(): jnp.sum(jnp.where(holder[:, None] == group_ids[None, :], block_order[None...  11.9 us
  transfers between devices with their start and end apart: 4, of which 4 were waited for; matrix products, arithmetic and copies ran while one was open for 2% of the time, Pallas kernels for 0%

commit v1 on v0

v1 whole, which is shorter than its diff:
```python
import functools

import jax
import jax.numpy as jnp
from jax import lax
from jax.experimental import pallas as pl
from jax.experimental.pallas import tpu as pltpu
from jax.sharding import PartitionSpec as P

MESH = pl.DeviceIdType.MESH
HEAD = 128
QPK = 4
ROWS = 256
PAGE = 16
COLS = 1024
SLOTS = 64
NPAGES = 512
NEG = -1e30
SCALE2 = 128.0 ** -0.5 * 1.4426950408889634

Z_SET = (1, 2, 4, 5, 7, 8, 9, 11, 12, 14, 15)
X_SET = (3, 6, 10, 13)
N_SET = 16

GROUP = 32
Y_FIRST = 5
X_FIRST = 3


def plus_slot(r):
    return 4 * Z_SET[r]


def minus_slot(r):
    return 4 * Z_SET[r] + 1


def x_slot(i):
    return 4 * X_SET[i // 2] + i % 2


def half_blocks(z, xl, c):
    def index(dz, other, flip):
        return lax.rem(z + dz + 8, 8) * 4 + (1 - xl if other else xl) * 2 + (1 - c if flip else c)

    found = []
    for flip in (0, 1):
        at = 2 * flip
        found += [(at, index(0, 0, flip), 0), (at + 1, index(0, 0, flip), 1)]
        for r in range(11):
            d = r // 3 + 1
            if r < 9:
                half, other = ((0, 0), (1, 0), (0, 1))[r % 3]
            else:
                half, other = (0, r - 9)
            found.append((plus_slot(r) + at, index(-d, other, flip), half))
            if r < 9:
                half, other = ((1, 0), (0, 0), (0, 1))[r % 3]
            else:
                half, other = (1, r - 9)
            found.append((minus_slot(r) + at, index(d, other, flip), half))
        for i, (dz, half) in enumerate(((0, 0), (0, 1), (1, 1), (-1, 1), (2, 1), (-2, 1), (3, 1), (-3, 1))):
            found.append((x_slot(i) + at, index(dz, 1, flip), half))
    return found


def kernel(order_ref, owner_ref, q_hbm, k_hbm, v_hbm, w_hbm, out_ref, pages_ref,
           kv, q_raw, qx, top, acc, att, w, part, uy, ux, wx, wy, table_v, table_s, place, holder,
           load_sem, w_sem, z_ssem, z_rsem, x_ssem, x_rsem, d_ssem, d_rsem,
           uy_ssem, uy_rsem, ux_ssem, ux_rsem, wx_ssem, wx_rsem, wy_ssem, wy_rsem):
    grp, tp = lax.axis_index("grp"), lax.axis_index("tp")
    z, xl, c = grp // 4, lax.rem(grp // 2, 2), lax.rem(grp, 2)
    y, xh = tp // 2, lax.rem(tp, 2)

    def at_grp(z_to, xl_to, c_to):
        return (z_to * 4 + xl_to * 2 + c_to, tp)

    z_up = at_grp(lax.rem(z + 1, 8), xl, c)
    z_down = at_grp(lax.rem(z + 7, 8), xl, c)
    x_near = at_grp(z, 1 - xl, c)
    core = at_grp(z, xl, 1 - c)
    y_up = (grp, lax.rem(y + 1, 4) * 2 + xh)
    y_down = (grp, lax.rem(y + 3, 4) * 2 + xh)
    x_far = (grp, y * 2 + 1 - xh)

    loads = []
    for half in range(2):
        for ref, lane in ((k_hbm, 0), (v_hbm, HEAD)):
            loads.append(pltpu.make_async_copy(
                ref.at[pl.ds(8 * half, 8)], kv.at[pl.ds(8 * half, 8), :, pl.ds(lane, HEAD)],
                load_sem.at[len(loads)]))
    load_q = pltpu.make_async_copy(q_hbm, q_raw, load_sem.at[4])
    load_w = pltpu.make_async_copy(w_hbm, w, w_sem)
    for load in loads:
        load.start()
    load_q.start()
    load_w.start()

    barrier = pltpu.get_barrier_semaphore()
    for near in (z_up, z_down, x_near, core, y_up, y_down, x_far):
        pl.semaphore_signal(barrier, inc=1, device_id=near, device_id_type=MESH)

    here = order_ref[grp]
    for slot, block, half in half_blocks(z, xl, c):
        place[2 * block + half] = slot + 0 * grp
        holder[slot] = block

    for load in loads:
        load.wait()
    pl.semaphore_wait(barrier, 7)

    sent = []

    def remote(src, dst, ssem, rsem, to):
        return pltpu.make_async_remote_copy(src_ref=src, dst_ref=dst, send_sem=ssem, recv_sem=rsem,
                                            device_id=to, device_id_type=MESH)

    def slots(first, count=1):
        return kv.at[pl.ds(8 * first, 8 * count)]

    def plus(r, src):
        return remote(slots(src), slots(plus_slot(r)), z_ssem.at[0, r], z_rsem.at[0, r], z_up)

    def minus(r, src):
        return remote(slots(src), slots(minus_slot(r)), z_ssem.at[1, r], z_rsem.at[1, r], z_down)

    def cross(i, src):
        return remote(slots(src), slots(x_slot(i)), x_ssem.at[i], x_rsem.at[i], x_near)

    def twin(k):
        return remote(slots(4 * k, 2), slots(4 * k + 2, 2), d_ssem.at[k], d_rsem.at[k], core)

    def begin(make, *which):
        make(*which).start()
        sent.append((make, which))

    begin(cross, 0, 0)
    begin(plus, 0, 0)
    begin(minus, 0, 1)
    begin(twin, 0)
    begin(cross, 1, 1)
    begin(plus, 1, 1)
    begin(minus, 1, 0)

    def z_step(r):
        plus(r, 0).wait_recv()
        minus(r, 0).wait_recv()
        if r <= 6:
            begin(plus, r + 3, plus_slot(r))
            begin(minus, r + 3, minus_slot(r))
        if r == 8:
            begin(plus, 10, plus_slot(8))
        if r % 3 == 0 and r <= 6:
            begin(cross, 2 + 2 * (r // 3), minus_slot(r))
        if r % 3 == 1 and r <= 7:
            begin(cross, 3 + 2 * (r // 3), plus_slot(r))
        begin(twin, Z_SET[r])

    def x_step(i):
        cross(i, 0).wait_recv()
        if i == 0:
            begin(plus, 2, x_slot(0))
            begin(minus, 2, x_slot(0))
        if i == 6:
            begin(minus, 10, x_slot(6))
        if i % 2 == 1:
            begin(twin, X_SET[i // 2])

    before = {
        1: (("z", 0), ("z", 1), ("x", 1)),
        2: (("z", 2),),
        4: (("z", 3), ("x", 2)),
        5: (("z", 4), ("x", 3)),
        7: (("z", 5),),
        8: (("z", 6), ("x", 4)),
        9: (("z", 7), ("x", 5)),
        11: (("z", 8), ("x", 6)),
        12: (("z", 9), ("x", 7)),
        14: (("z", 10),),
    }

    def softmax_step(k, first):
        block = kv[pl.ds(32 * k, 32)].reshape(512, 2 * HEAD)
        rows = []
        for j in range(4):
            seen = order_ref[holder[4 * k + j]] < here
            if first and j < 2:
                seen = True
            rows.append(jnp.full((HEAD, HEAD), jnp.where(seen, 0.0, NEG), jnp.float32).astype(jnp.bfloat16))
        keys = jnp.concatenate([block[:, :HEAD], jnp.concatenate(rows, axis=0)], axis=1)
        values = jnp.concatenate([block[:, HEAD:], jnp.ones((512, HEAD), jnp.bfloat16)], axis=1)
        for h in range(QPK):
            scores = lax.dot_general(qx[h], keys, (((1,), (1,)), ((), ())), preferred_element_type=jnp.float32)
            tiles = [scores[:, HEAD * j:HEAD * (j + 1)] for j in range(4)]
            if first:
                row = lax.broadcasted_iota(jnp.int32, (ROWS, HEAD), 0)
                lane = lax.broadcasted_iota(jnp.int32, (ROWS, HEAD), 1)
                for j in range(2):
                    tiles[j] = jnp.where(lane + HEAD * j <= row, tiles[j], NEG)
            peak = jnp.max(jnp.maximum(jnp.maximum(tiles[0], tiles[1]), jnp.maximum(tiles[2], tiles[3])),
                           axis=1, keepdims=True)
            if first:
                new = jnp.broadcast_to(peak, (ROWS, HEAD))
            else:
                old = top[h]
                new = jnp.maximum(old, peak)
            expo = [jnp.exp2((tile - new) * SCALE2).astype(jnp.bfloat16) for tile in tiles]
            gained = jnp.dot(jnp.concatenate(expo, axis=1), values, preferred_element_type=jnp.float32)
            top[h] = new
            if first:
                acc[h] = gained
            else:
                factor = jnp.exp2((old - new) * SCALE2)
                acc[h] = acc[h] * jnp.concatenate([factor, factor], axis=1) + gained

    load_q.wait()
    lane = lax.broadcasted_iota(jnp.int32, (ROWS, HEAD), 1)
    unit = jnp.where(lane == 0, 1.0, 0.0).astype(jnp.bfloat16)
    for h in range(QPK):
        qx[h] = jnp.concatenate([q_raw[:, HEAD * h:HEAD * (h + 1)], unit], axis=1)
    x_step(0)
    twin(0).wait_recv()
    softmax_step(0, True)

    @pl.loop(1, N_SET)
    def _(k):
        for at, events in before.items():
            @pl.when(k == at)
            def _():
                for kind, r in events:
                    (z_step if kind == "z" else x_step)(r)
        twin(k).wait_recv()
        softmax_step(k, False)

    for h in range(QPK):
        att[:, HEAD * h:HEAD * (h + 1)] = (acc[h, :, :HEAD] / acc[h, :, HEAD:]).astype(jnp.bfloat16)
    load_w.wait()

    def project(i, j):
        first = (lax.rem(y + i, 4) * 2 + (1 - xh if j else xh)) * COLS

        @pl.loop(0, 4)
        def _(n):
            at = pl.multiple_of(first + n * 256, 256)
            to = pl.multiple_of(n * 256, 256)
            part[i, j, :, pl.ds(to, 256)] = jnp.dot(
                att[...], w[:, pl.ds(at, 256)], preferred_element_type=jnp.float32).astype(jnp.bfloat16)

    def rows_of(g):
        return pl.ds(g * GROUP, GROUP)

    def near_y(g, way, n, src=None):
        i, j = ((2, 0), (1, 1), (1, 0))[n] if way == 0 else ((2, 1), (3, 0), (3, 1))[n]
        return remote(part.at[i, j, rows_of(g)], uy.at[g, way, n], uy_ssem.at[g, way, n], uy_rsem.at[g, way, n],
                      (y_up, y_down)[way])

    def far_x(g):
        return remote(part.at[0, 1, rows_of(g)], ux.at[g], ux_ssem.at[g], ux_rsem.at[g], x_far)

    def far_first(g, i):
        return remote(part.at[i, 1, rows_of(Y_FIRST + g)], wx.at[g, i], wx_ssem.at[g, i], wx_rsem.at[g, i], x_far)

    def near_last(g, way, n):
        i = (2, 1, 1)[n] if way == 0 else (2, 3, 3)[n]
        left = (0, 1, 0)[n] if way == 0 else (1, 0, 1)[n]
        return remote(part.at[i, 0, rows_of(Y_FIRST + g), pl.ds(512 * left, 512)], wy.at[g, way, n],
                      wy_ssem.at[g, way, n], wy_rsem.at[g, way, n], (y_up, y_down)[way])

    def wide(a):
        return a.astype(jnp.float32)

    def u_begin(g):
        for n in (0, 1):
            for way in (0, 1):
                begin(near_y, g, way, n)

    def u_add(g):
        for way, i, j in ((0, 1, 0), (1, 3, 1)):
            near_y(g, way, 0).wait_recv()
            part[i, j, rows_of(g)] = (wide(part[i, j, rows_of(g)]) + wide(uy[g, way, 0])).astype(jnp.bfloat16)
            begin(near_y, g, way, 2)

    def u_total(g, j):
        return wide(part[0, j, rows_of(g)]) + wide(uy[g, 0, 2 - j]) + wide(uy[g, 1, 1 + j])

    def u_cross(g):
        for way in (0, 1):
            for n in (1, 2):
                near_y(g, way, n).wait_recv()
        part[0, 1, rows_of(g)] = u_total(g, 1).astype(jnp.bfloat16)
        begin(far_x, g)

    def u_out(g):
        far_x(g).wait_recv()
        out_ref[rows_of(g)] = (u_total(g, 0) + wide(ux[g])).astype(jnp.bfloat16)

    def w_begin(g):
        for i in (2, 1, 3, 0):
            begin(far_first, g, i)

    def w_mid(g):
        at = rows_of(Y_FIRST + g)
        for i in (2, 1, 3):
            far_first(g, i).wait_recv()
            part[i, 0, at] = (wide(part[i, 0, at]) + wide(wx[g, i])).astype(jnp.bfloat16)
            if i == 2:
                begin(near_last, g, 0, 0)
                begin(near_last, g, 1, 0)
            else:
                begin(near_last, g, (1 if i == 3 else 0), 1)

    def w_add(g):
        at = rows_of(Y_FIRST + g)
        for way, i in ((0, 1), (1, 3)):
            near_last(g, way, 0).wait_recv()
            cols = pl.ds(512 * way, 512)
            part[i, 0, at, cols] = (wide(part[i, 0, at, cols]) + wide(wy[g, way, 0])).astype(jnp.bfloat16)
            begin(near_last, g, way, 2)

    def w_out(g):
        at = rows_of(Y_FIRST + g)
        far_first(g, 0).wait_recv()
        for way in (0, 1):
            for n in (1, 2):
                near_last(g, way, n).wait_recv()
        total = wide(part[0, 0, at]) + wide(wx[g, 0])
        came = [wide(wy[g, 0, 2 - left]) + wide(wy[g, 1, 1 + left]) for left in (0, 1)]
        out_ref[at] = (total + jnp.concatenate(came, axis=1)).astype(jnp.bfloat16)

    def hand_pages():
        lanes = lax.broadcasted_iota(jnp.int32, (8, 128), 1)

        def look(i, carry):
            found, count = carry
            mine = owner_ref[i] == grp
            found = jnp.where((lanes == count) & mine, i, found)
            return found, count + jnp.where(mine, 1, 0)

        found, count = lax.fori_loop(0, NPAGES, look, (jnp.zeros((8, 128), jnp.int32), 0 * grp), unroll=8)
        table_v[...] = found
        fetch = pltpu.make_async_copy(table_v, table_s, load_sem.at[5])
        fetch.start()
        fetch.wait()

        @pl.loop(0, SLOTS)
        def _(s):
            page = table_s[0, s]
            slot = place[page // 8]
            rows = kv[slot * 8 + lax.rem(page, 8)]
            pages_ref[s] = jnp.where(s < count, rows, jnp.zeros_like(rows))

    project(2, 0)
    begin(near_y, 0, 0, 0)
    project(2, 1)
    begin(near_y, 0, 1, 0)
    begin(far_first, 0, 2)
    project(1, 1)
    begin(near_y, 0, 0, 1)
    begin(far_first, 0, 1)
    project(3, 0)
    begin(near_y, 0, 1, 1)
    project(3, 1)
    begin(far_first, 0, 3)
    project(0, 1)
    begin(far_first, 0, 0)
    project(1, 0)
    u_begin(1)
    u_add(0)
    project(0, 0)
    w_begin(1)
    hand_pages()
    u_begin(2)
    u_add(1)
    u_cross(0)
    w_mid(0)
    w_begin(2)
    u_begin(3)
    u_add(2)
    u_cross(1)
    w_add(0)
    u_out(0)
    u_begin(4)
    u_add(3)
    u_cross(2)
    w_mid(1)
    u_out(1)
    w_out(0)
    u_add(4)
    u_cross(3)
    w_add(1)
    w_mid(2)
    u_out(2)
    u_cross(4)
    w_add(2)
    w_out(1)
    u_out(3)
    w_out(2)
    u_out(4)

    for make, which in sent:
        make(*which).wait_send()


def on_device(queries, key_rows, value_rows, out_weight, block_order, page_owner):
    dma = pltpu.SemaphoreType.DMA
    vmem = pltpu.VMEM
    bf16, f32, i32 = jnp.bfloat16, jnp.float32, jnp.int32
    smem_in = pl.BlockSpec(memory_space=pltpu.SMEM)
    hbm_in = pl.BlockSpec(memory_space=pl.ANY)
    vmem_out = pl.BlockSpec(memory_space=pltpu.VMEM)
    return pl.pallas_call(
        kernel,
        name="attend",
        out_shape=(jax.ShapeDtypeStruct((ROWS, COLS), bf16),
                   jax.ShapeDtypeStruct((SLOTS, PAGE, 2 * HEAD), bf16)),
        in_specs=[smem_in, smem_in, hbm_in, hbm_in, hbm_in, hbm_in],
        out_specs=(vmem_out, vmem_out),
        scratch_shapes=[
            vmem((NPAGES, PAGE, 2 * HEAD), bf16),
            vmem((ROWS, QPK * HEAD), bf16),
            vmem((QPK, ROWS, 2 * HEAD), bf16),
            vmem((QPK, ROWS, HEAD), f32),
            vmem((QPK, ROWS, 2 * HEAD), f32),
            vmem((ROWS, QPK * HEAD), bf16),
            vmem((QPK * HEAD, 8 * COLS), bf16),
            vmem((4, 2, ROWS, COLS), bf16),
            vmem((Y_FIRST, 2, 3, GROUP, COLS), bf16),
            vmem((Y_FIRST, GROUP, COLS), bf16),
            vmem((X_FIRST, 4, GROUP, COLS), bf16),
            vmem((X_FIRST, 2, 3, GROUP, COLS // 2), bf16),
            vmem((8, 128), i32),
            pltpu.SMEM((8, 128), i32),
            pltpu.SMEM((64,), i32),
            pltpu.SMEM((64,), i32),
            dma((6,)), dma,
            dma((2, 11)), dma((2, 11)), dma((8,)), dma((8,)), dma((N_SET,)), dma((N_SET,)),
            dma((Y_FIRST, 2, 3)), dma((Y_FIRST, 2, 3)), dma((Y_FIRST,)), dma((Y_FIRST,)),
            dma((X_FIRST, 4)), dma((X_FIRST, 4)), dma((X_FIRST, 2, 3)), dma((X_FIRST, 2, 3)),
        ],
        compiler_params=pltpu.CompilerParams(
            collective_id=0, has_side_effects=True, vmem_limit_bytes=56 * 2**20),
    )(block_order, page_owner.reshape(NPAGES), queries,
      key_rows.reshape(PAGE, PAGE, HEAD), value_rows.reshape(PAGE, PAGE, HEAD), out_weight)


def solution(mesh):
    placed = (P("grp", "tp"), P("grp", "tp"), P("grp", "tp"), P("tp", None), P(), P())
    return jax.shard_map(
        on_device,
        mesh=mesh,
        in_specs=placed,
        out_specs=(P("grp", "tp"), P("grp", None, "tp")),
        check_vma=False,
    )
```

time: 390 us -> 78.2 us (0.20)
  waiting for transfers between devices: 215 us -> 0 us
  Pallas kernels: 0 us -> 73.6 us
  other arithmetic: 49.1 us -> 0 us
  starting transfers between devices: 44.7 us -> 0 us
  matrix products: 27.2 us -> 0 us
  loops' own time: 22.2 us -> 0 us
  between operations: 14.5 us -> 0.64 us
  local copies, waits for them, and re-layouts: 16 us -> 3.74 us
    all_gather x2 -> x0, waiting for transfers between devices: 131 us -> none  [the longest x1 66.3 us: on_device(): value_piece = lax.all_gather(value_rows, 'grp', axis=0, tiled=True)]
    pallas_call x0 -> x1, Pallas kernels: none -> 73.6 us  [on_device(): pl.pallas_call(kernel, name='attend', out_shape=(jax.ShapeDtypeStruct((RO...]
    reduce_scatter x1 -> x0, waiting for transfers between devices: 64.9 us -> none  [on_device(): lax.psum_scatter(partial_term.astype(jnp.bfloat16), 'tp', scatter_dimensi...]
    all_to_all x1 -> x0, starting transfers between devices: 44.6 us -> none  [on_device(): lax.all_to_all(outgoing, 'grp', split_axis=0, concat_axis=0, tiled=True)]
    dot_general x15 -> x0, matrix products: 27.2 us -> none  [the longest x6 10.6 us: softmax_update(): jnp.einsum('hck,kd->hcd', weights, value_tile, preferred_element_type=jnp...]
    another operation x17 -> x0, loops' own time: 22.2 us -> none  [the longest x1 21.6 us: on_device(): lax.scan(one_step, running, (key_blocks, value_blocks, offsets))]
    reduce_min x16 -> x0, other arithmetic: 21.2 us -> none  [one_step(): state_now = lax.cond(jnp.min(key_pos) > top_query, keep, compute, state_now)]
    all_to_all x1 -> x0, waiting for transfers between devices: 17.5 us -> none  [on_device(): lax.all_to_all(outgoing, 'grp', split_axis=0, concat_axis=0, tiled=True)]
  transfers between devices with their start and end apart: 4 -> 0, of which waited for: 4 -> 0; matrix products, arithmetic and copies ran while one was open for 2% -> 0% of each run, Pallas kernels for 0% -> 0%
where the time goes in v1:
time: 78.2 us; the launch traced here: 78 us
  Pallas kernels  73.6 us (94%)
  local copies, waits for them, and re-layouts  3.74 us (5%)
    pallas_call x1, Pallas kernels, on_device(): pl.pallas_call(kernel, name='attend', out_shape=(jax.ShapeDtypeStruct((RO...  73.6 us
    unnamed x2, local copies, waits for them, and re-layouts  3.74 us

profile of v1, /device:TPU:8, one launch (start us, length us, event | category | flops | bytes accessed | tf_op | source)
XLA Modules:
  0.0 78.0 jit_solution(7041196011029138595)
XLA Ops:
  0.6 73.6 %attend.1 = (bf16[256,1024]{1,0:T(8,128)(2,1)}, bf16[64,16,256]{2,1,0:T(8,128)(2,1)}) custom-call(s32[32]{0:T(128)} %order_ref.1, s32[512]{0:T(512)} %bitcast.5, bf16[256,512]{1,0:T(8,128)(2,1)} %q_hbm.1, bf16[16,16,128]{2,1,0:T(8,128)(2,1)} %bitcast.3, bf16[16,16,128]{2,1,0:T(8,128)(2,1)} %bitcast.4, bf16[512,8192]{1,0:T(8,128)(2,1)} %w_hbm.1), custom_call_target="tpu_custom_call" | custom-call | tf_op jit(solution)/shard_map/attend/pallas_call | solution.py:411
  74.3 1.9 %copy.10 = bf16[256,1024]{1,0:T(8,128)(2,1)} copy(bf16[256,1024]{1,0:T(8,128)(2,1)} %get-tuple-element.4) | data formatting | bytes 1048576
  76.1 1.9 %copy.11 = bf16[64,16,256]{2,1,0:T(8,128)(2,1)} copy(bf16[64,16,256]{2,1,0:T(8,128)(2,1)} %get-tuple-element.5) | data formatting | bytes 1048576

commit v2 on v1

--- a/solution.py
+++ b/solution.py
@@ -18,13 +18,27 @@
 NEG = -1e30
 SCALE2 = 128.0 ** -0.5 * 1.4426950408889634
 
-Z_SET = (1, 2, 4, 5, 7, 8, 9, 11, 12, 14, 15)
-X_SET = (3, 6, 10, 13)
+Z_SET = (1, 3, 4, 5, 7, 8, 9, 10, 12, 13, 15)
+X_SET = (2, 6, 11, 14)
 N_SET = 16
 
-GROUP = 32
-Y_FIRST = 5
-X_FIRST = 3
+Y_ROWS = (48, 48, 48)
+X_ROWS = (48, 64)
+Y_FIRST, X_FIRST = len(Y_ROWS), len(X_ROWS)
+ORDER = (
+    ("p", 2, 0), ("s", "y", 0, 0, 0), ("p", 2, 1), ("s", "y", 0, 1, 0), ("s", "x", 0, 2),
+    ("p", 1, 1), ("s", "y", 0, 0, 1), ("s", "y", 1, 0, 0), ("s", "y", 1, 0, 1), ("s", "y", 2, 0, 0),
+    ("s", "y", 2, 0, 1), ("s", "x", 0, 1),
+    ("p", 3, 0), ("s", "y", 0, 1, 1), ("s", "y", 1, 1, 0), ("s", "y", 1, 1, 1), ("s", "y", 2, 1, 0),
+    ("s", "y", 2, 1, 1),
+    ("p", 3, 1), ("s", "x", 0, 3),
+    ("p", 0, 1), ("s", "x", 0, 0), ("s", "x", 1, 2), ("s", "x", 1, 1), ("s", "x", 1, 3), ("s", "x", 1, 0),
+    ("p", 1, 0), ("p", 0, 0),
+    ("ua", 0, 0), ("ua", 0, 1), ("wm", 0, 2), ("pages", 0), ("pages", 1), ("wm", 0, 1), ("pages", 2),
+    ("ua", 1, 0), ("ua", 1, 1), ("wm", 0, 3), ("pages", 3), ("ua", 2, 0), ("ua", 2, 1),
+    ("wm", 1, 2), ("wm", 1, 1), ("uc", 0), ("wa", 0, 0), ("wa", 0, 1), ("wm", 1, 3), ("uc", 1), ("uc", 2),
+    ("wa", 1, 0), ("uo", 0), ("wa", 1, 1), ("uo", 1), ("wo", 0), ("wo", 1), ("uo", 2),
+)
 
 
 def plus_slot(r):
@@ -167,16 +181,17 @@
             begin(twin, X_SET[i // 2])
 
     before = {
-        1: (("z", 0), ("z", 1), ("x", 1)),
-        2: (("z", 2),),
-        4: (("z", 3), ("x", 2)),
-        5: (("z", 4), ("x", 3)),
-        7: (("z", 5),),
-        8: (("z", 6), ("x", 4)),
-        9: (("z", 7), ("x", 5)),
-        11: (("z", 8), ("x", 6)),
-        12: (("z", 9), ("x", 7)),
-        14: (("z", 10),),
+        1: (("x", 0), ("z", 0), ("x", 1), ("z", 1)),
+        3: (("z", 2), ("x", 2)),
+        4: (("z", 3), ("x", 3)),
+        5: (("z", 4),),
+        6: (("z", 5),),
+        7: (("z", 6), ("x", 4)),
+        8: (("x", 5), ("z", 7)),
+        10: (("z", 8), ("x", 6)),
+        11: (("z", 9),),
+        12: (("x", 7),),
+        13: (("z", 10),),
     }
 
     def softmax_step(k, first):
@@ -189,9 +204,10 @@
             rows.append(jnp.full((HEAD, HEAD), jnp.where(seen, 0.0, NEG), jnp.float32).astype(jnp.bfloat16))
         keys = jnp.concatenate([block[:, :HEAD], jnp.concatenate(rows, axis=0)], axis=1)
         values = jnp.concatenate([block[:, HEAD:], jnp.ones((512, HEAD), jnp.bfloat16)], axis=1)
+        scores = [lax.dot_general(qx[h], keys, (((1,), (1,)), ((), ())), preferred_element_type=jnp.float32)
+                  for h in range(QPK)]
         for h in range(QPK):
-            scores = lax.dot_general(qx[h], keys, (((1,), (1,)), ((), ())), preferred_element_type=jnp.float32)
-            tiles = [scores[:, HEAD * j:HEAD * (j + 1)] for j in range(4)]
+            tiles = [scores[h][:, HEAD * j:HEAD * (j + 1)] for j in range(4)]
             if first:
                 row = lax.broadcasted_iota(jnp.int32, (ROWS, HEAD), 0)
                 lane = lax.broadcasted_iota(jnp.int32, (ROWS, HEAD), 1)
@@ -218,7 +234,6 @@
     unit = jnp.where(lane == 0, 1.0, 0.0).astype(jnp.bfloat16)
     for h in range(QPK):
         qx[h] = jnp.concatenate([q_raw[:, HEAD * h:HEAD * (h + 1)], unit], axis=1)
-    x_step(0)
     twin(0).wait_recv()
     softmax_step(0, True)
 
@@ -246,88 +261,84 @@
             part[i, j, :, pl.ds(to, 256)] = jnp.dot(
                 att[...], w[:, pl.ds(at, 256)], preferred_element_type=jnp.float32).astype(jnp.bfloat16)
 
-    def rows_of(g):
-        return pl.ds(g * GROUP, GROUP)
-
-    def near_y(g, way, n, src=None):
+    def u_rows(g):
+        return pl.ds(sum(Y_ROWS[:g]), Y_ROWS[g])
+
+    def w_rows(g):
+        return pl.ds(sum(Y_ROWS) + sum(X_ROWS[:g]), X_ROWS[g])
+
+    def u_near(g, way, n):
         i, j = ((2, 0), (1, 1), (1, 0))[n] if way == 0 else ((2, 1), (3, 0), (3, 1))[n]
-        return remote(part.at[i, j, rows_of(g)], uy.at[g, way, n], uy_ssem.at[g, way, n], uy_rsem.at[g, way, n],
-                      (y_up, y_down)[way])
-
-    def far_x(g):
-        return remote(part.at[0, 1, rows_of(g)], ux.at[g], ux_ssem.at[g], ux_rsem.at[g], x_far)
-
-    def far_first(g, i):
-        return remote(part.at[i, 1, rows_of(Y_FIRST + g)], wx.at[g, i], wx_ssem.at[g, i], wx_rsem.at[g, i], x_far)
-
-    def near_last(g, way, n):
+        return remote(part.at[i, j, u_rows(g)], uy.at[g, way, n, pl.ds(0, Y_ROWS[g])],
+                      uy_ssem.at[g, way, n], uy_rsem.at[g, way, n], (y_up, y_down)[way])
+
+    def u_far(g):
+        return remote(part.at[0, 1, u_rows(g)], ux.at[g, pl.ds(0, Y_ROWS[g])], ux_ssem.at[g], ux_rsem.at[g], x_far)
+
+    def w_far(g, i):
+        return remote(part.at[i, 1, w_rows(g)], wx.at[g, i, pl.ds(0, X_ROWS[g])],
+                      wx_ssem.at[g, i], wx_rsem.at[g, i], x_far)
+
+    def w_near(g, way, n):
         i = (2, 1, 1)[n] if way == 0 else (2, 3, 3)[n]
         left = (0, 1, 0)[n] if way == 0 else (1, 0, 1)[n]
-        return remote(part.at[i, 0, rows_of(Y_FIRST + g), pl.ds(512 * left, 512)], wy.at[g, way, n],
+        return remote(part.at[i, 0, w_rows(g), pl.ds(512 * left, 512)], wy.at[g, way, n, pl.ds(0, X_ROWS[g])],
                       wy_ssem.at[g, way, n], wy_rsem.at[g, way, n], (y_up, y_down)[way])
 
     def wide(a):
         return a.astype(jnp.float32)
 
-    def u_begin(g):
-        for n in (0, 1):
-            for way in (0, 1):
-                begin(near_y, g, way, n)
-
-    def u_add(g):
-        for way, i, j in ((0, 1, 0), (1, 3, 1)):
-            near_y(g, way, 0).wait_recv()
-            part[i, j, rows_of(g)] = (wide(part[i, j, rows_of(g)]) + wide(uy[g, way, 0])).astype(jnp.bfloat16)
-            begin(near_y, g, way, 2)
+    def u_add(g, way):
+        i, j = ((1, 0), (3, 1))[way]
+        u_near(g, way, 0).wait_recv()
+        came = uy[g, way, 0, :Y_ROWS[g]]
+        part[i, j, u_rows(g)] = (wide(part[i, j, u_rows(g)]) + wide(came)).astype(jnp.bfloat16)
+        begin(u_near, g, way, 2)
 
     def u_total(g, j):
-        return wide(part[0, j, rows_of(g)]) + wide(uy[g, 0, 2 - j]) + wide(uy[g, 1, 1 + j])
+        size = Y_ROWS[g]
+        return wide(part[0, j, u_rows(g)]) + wide(uy[g, 0, 2 - j, :size]) + wide(uy[g, 1, 1 + j, :size])
 
     def u_cross(g):
         for way in (0, 1):
             for n in (1, 2):
-                near_y(g, way, n).wait_recv()
-        part[0, 1, rows_of(g)] = u_total(g, 1).astype(jnp.bfloat16)
-        begin(far_x, g)
+                u_near(g, way, n).wait_recv()
+        part[0, 1, u_rows(g)] = u_total(g, 1).astype(jnp.bfloat16)
+        begin(u_far, g)
 
     def u_out(g):
-        far_x(g).wait_recv()
-        out_ref[rows_of(g)] = (u_total(g, 0) + wide(ux[g])).astype(jnp.bfloat16)
-
-    def w_begin(g):
-        for i in (2, 1, 3, 0):
-            begin(far_first, g, i)
-
-    def w_mid(g):
-        at = rows_of(Y_FIRST + g)
-        for i in (2, 1, 3):
-            far_first(g, i).wait_recv()
-            part[i, 0, at] = (wide(part[i, 0, at]) + wide(wx[g, i])).astype(jnp.bfloat16)
-            if i == 2:
-                begin(near_last, g, 0, 0)
-                begin(near_last, g, 1, 0)
-            else:
-                begin(near_last, g, (1 if i == 3 else 0), 1)
-
-    def w_add(g):
-        at = rows_of(Y_FIRST + g)
-        for way, i in ((0, 1), (1, 3)):
-            near_last(g, way, 0).wait_recv()
-            cols = pl.ds(512 * way, 512)
-            part[i, 0, at, cols] = (wide(part[i, 0, at, cols]) + wide(wy[g, way, 0])).astype(jnp.bfloat16)
-            begin(near_last, g, way, 2)
+        u_far(g).wait_recv()
+        out_ref[u_rows(g)] = (u_total(g, 0) + wide(ux[g, :Y_ROWS[g]])).astype(jnp.bfloat16)
+
+    def w_mid(g, i):
+        at = w_rows(g)
+        w_far(g, i).wait_recv()
+        part[i, 0, at] = (wide(part[i, 0, at]) + wide(wx[g, i, :X_ROWS[g]])).astype(jnp.bfloat16)
+        if i == 2:
+            begin(w_near, g, 0, 0)
+            begin(w_near, g, 1, 0)
+        else:
+            begin(w_near, g, (1 if i == 3 else 0), 1)
+
+    def w_add(g, way):
+        at, cols = w_rows(g), pl.ds(512 * way, 512)
+        i = (1, 3)[way]
+        w_near(g, way, 0).wait_recv()
+        came = wy[g, way, 0, :X_ROWS[g]]
+        part[i, 0, at, cols] = (wide(part[i, 0, at, cols]) + wide(came)).astype(jnp.bfloat16)
+        begin(w_near, g, way, 2)
 
     def w_out(g):
-        at = rows_of(Y_FIRST + g)
-        far_first(g, 0).wait_recv()
+        at, size = w_rows(g), X_ROWS[g]
+        w_far(g, 0).wait_recv()
         for way in (0, 1):
             for n in (1, 2):
-                near_last(g, way, n).wait_recv()
-        total = wide(part[0, 0, at]) + wide(wx[g, 0])
-        came = [wide(wy[g, 0, 2 - left]) + wide(wy[g, 1, 1 + left]) for left in (0, 1)]
+                w_near(g, way, n).wait_recv()
+        total = wide(part[0, 0, at]) + wide(wx[g, 0, :size])
+        came = [wide(wy[g, 0, 2 - left, :size]) + wide(wy[g, 1, 1 + left, :size]) for left in (0, 1)]
         out_ref[at] = (total + jnp.concatenate(came, axis=1)).astype(jnp.bfloat16)
 
-    def hand_pages():
+    def find_pages():
         lanes = lax.broadcasted_iota(jnp.int32, (8, 128), 1)
 
         def look(i, carry):
@@ -341,64 +352,36 @@
         fetch = pltpu.make_async_copy(table_v, table_s, load_sem.at[5])
         fetch.start()
         fetch.wait()
-
-        @pl.loop(0, SLOTS)
+        return count
+
+    def hand_pages(first, count):
+        @pl.loop(first, first + SLOTS // 4)
         def _(s):
             page = table_s[0, s]
             slot = place[page // 8]
             rows = kv[slot * 8 + lax.rem(page, 8)]
             pages_ref[s] = jnp.where(s < count, rows, jnp.zeros_like(rows))
 
-    project(2, 0)
-    begin(near_y, 0, 0, 0)
-    project(2, 1)
-    begin(near_y, 0, 1, 0)
-    begin(far_first, 0, 2)
-    project(1, 1)
-    begin(near_y, 0, 0, 1)
-    begin(far_first, 0, 1)
-    project(3, 0)
-    begin(near_y, 0, 1, 1)
-    project(3, 1)
-    begin(far_first, 0, 3)
-    project(0, 1)
-    begin(far_first, 0, 0)
-    project(1, 0)
-    u_begin(1)
-    u_add(0)
-    project(0, 0)
-    w_begin(1)
-    hand_pages()
-    u_begin(2)
-    u_add(1)
-    u_cross(0)
-    w_mid(0)
-    w_begin(2)
-    u_begin(3)
-    u_add(2)
-    u_cross(1)
-    w_add(0)
-    u_out(0)
-    u_begin(4)
-    u_add(3)
-    u_cross(2)
-    w_mid(1)
-    u_out(1)
-    w_out(0)
-    u_add(4)
-    u_cross(3)
-    w_add(1)
-    w_mid(2)
-    u_out(2)
-    u_cross(4)
-    w_add(2)
-    w_out(1)
-    u_out(3)
-    w_out(2)
-    u_out(4)
+    owned = 0
+    for step, *which in ORDER:
+        if step == "p":
+            project(*which)
+        elif step == "s":
+            begin(u_near if which[0] == "y" else w_far, *which[1:])
+        elif step == "pages":
+            if which[0] == 0:
+                owned = find_pages()
+            hand_pages(which[0] * (SLOTS // 4), owned)
+        else:
+            {"ua": u_add, "uc": u_cross, "uo": u_out, "wm": w_mid, "wa": w_add, "wo": w_out}[step](*which)
 
     for make, which in sent:
         make(*which).wait_send()
+
+
+def hand_over(made, paged, out, pages):
+    out[...] = made[...]
+    pages[...] = paged[...]
 
 
 def on_device(queries, key_rows, value_rows, out_weight, block_order, page_owner):
@@ -408,7 +391,7 @@
     smem_in = pl.BlockSpec(memory_space=pltpu.SMEM)
     hbm_in = pl.BlockSpec(memory_space=pl.ANY)
     vmem_out = pl.BlockSpec(memory_space=pltpu.VMEM)
-    return pl.pallas_call(
+    made = pl.pallas_call(
         kernel,
         name="attend",
         out_shape=(jax.ShapeDtypeStruct((ROWS, COLS), bf16),
@@ -424,10 +407,10 @@
             vmem((ROWS, QPK * HEAD), bf16),
             vmem((QPK * HEAD, 8 * COLS), bf16),
             vmem((4, 2, ROWS, COLS), bf16),
-            vmem((Y_FIRST, 2, 3, GROUP, COLS), bf16),
-            vmem((Y_FIRST, GROUP, COLS), bf16),
-            vmem((X_FIRST, 4, GROUP, COLS), bf16),
-            vmem((X_FIRST, 2, 3, GROUP, COLS // 2), bf16),
+            vmem((Y_FIRST, 2, 3, max(Y_ROWS), COLS), bf16),
+            vmem((Y_FIRST, max(Y_ROWS), COLS), bf16),
+            vmem((X_FIRST, 4, max(X_ROWS), COLS), bf16),
+            vmem((X_FIRST, 2, 3, max(X_ROWS), COLS // 2), bf16),
             vmem((8, 128), i32),
             pltpu.SMEM((8, 128), i32),
             pltpu.SMEM((64,), i32),
@@ -441,6 +424,13 @@
             collective_id=0, has_side_effects=True, vmem_limit_bytes=56 * 2**20),
     )(block_order, page_owner.reshape(NPAGES), queries,
       key_rows.reshape(PAGE, PAGE, HEAD), value_rows.reshape(PAGE, PAGE, HEAD), out_weight)
+    return pl.pallas_call(
+        hand_over,
+        name="hand_over",
+        out_shape=tuple(jax.ShapeDtypeStruct(a.shape, a.dtype) for a in made),
+        in_specs=[vmem_out, vmem_out],
+        out_specs=(vmem_out, vmem_out),
+    )(*made)
 
 
 def solution(mesh):

time: 78.2 us -> 69.1 us (0.88)
  Pallas kernels: 73.6 us -> 68.3 us
  local copies, waits for them, and re-layouts: 3.74 us -> 0 us
    pallas_call x1, Pallas kernels: 73.6 us -> 66.1 us  [on_device(): pl.pallas_call(kernel, name='attend', out_shape=(jax.ShapeDtypeStruct((RO...]
    unnamed x2 -> x0, local copies, waits for them, and re-layouts: 3.74 us -> none
    pallas_call x0 -> x1, Pallas kernels: none -> 2.2 us  [on_device(): pl.pallas_call(hand_over, name='hand_over', out_shape=tuple((jax.ShapeDty...]
where the time goes in v2:
time: 69.1 us; the launch traced here: 69 us
  Pallas kernels  68.3 us (99%)
    pallas_call x1, Pallas kernels, on_device(): pl.pallas_call(kernel, name='attend', out_shape=(jax.ShapeDtypeStruct((RO...  66.1 us
    pallas_call x1, Pallas kernels, on_device(): pl.pallas_call(hand_over, name='hand_over', out_shape=tuple((jax.ShapeDty...  2.2 us

profile of v2, /device:TPU:8, one launch (start us, length us, event | category | flops | bytes accessed | tf_op | source)
XLA Modules:
  0.0 69.0 jit_solution(9598877121552296304)
XLA Ops:
  0.6 66.1 %attend.1 = (bf16[256,1024]{1,0:T(8,128)(2,1)}, bf16[64,16,256]{2,1,0:T(8,128)(2,1)}) custom-call(s32[32]{0:T(128)} %order_ref.1, s32[512]{0:T(512)} %bitcast.5, bf16[256,512]{1,0:T(8,128)(2,1)} %q_hbm.1, bf16[16,16,128]{2,1,0:T(8,128)(2,1)} %bitcast.3, bf16[16,16,128]{2,1,0:T(8,128)(2,1)} %bitcast.4, bf16[512,8192]{1,0:T(8,128)(2,1)} %w_hbm.1), custom_call_target="tpu_custom_call" | custom-call | tf_op jit(solution)/shard_map/attend/pallas_call | solution.py:394
  66.8 2.2 %hand_over.1 = (bf16[256,1024]{1,0:T(8,128)(2,1)}, bf16[64,16,256]{2,1,0:T(8,128)(2,1)}) custom-call(bf16[256,1024]{1,0:T(8,128)(2,1)} %get-tuple-element.4.made, bf16[64,16,256]{2,1,0:T(8,128)(2,1)} %get-tuple-element.5.paged), custom_call_target="tpu_custom_call" | custom-call | tf_op jit(solution)/shard_map/hand_over/pallas_call | solution.py:427

commit v3 on v2

--- a/solution.py
+++ b/solution.py
@@ -78,8 +78,8 @@
     return found
 
 
-def kernel(order_ref, owner_ref, q_hbm, k_hbm, v_hbm, w_hbm, out_ref, pages_ref,
-           kv, q_raw, qx, top, acc, att, w, part, uy, ux, wx, wy, table_v, table_s, place, holder,
+def kernel(order_hbm, owner_hbm, q_hbm, k_hbm, v_hbm, w_hbm, out_ref, pages_ref,
+           order_ref, owner_ref, kv, q_raw, qx, top, acc, att, w, part, uy, ux, wx, wy, table_v, table_s, place, holder,
            load_sem, w_sem, z_ssem, z_rsem, x_ssem, x_rsem, d_ssem, d_rsem,
            uy_ssem, uy_rsem, ux_ssem, ux_rsem, wx_ssem, wx_rsem, wy_ssem, wy_rsem):
     grp, tp = lax.axis_index("grp"), lax.axis_index("tp")
@@ -96,6 +96,10 @@
     y_up = (grp, lax.rem(y + 1, 4) * 2 + xh)
     y_down = (grp, lax.rem(y + 3, 4) * 2 + xh)
     x_far = (grp, y * 2 + 1 - xh)
+
+    barrier = pltpu.get_barrier_semaphore()
+    for near in (z_up, z_down, x_near, core, y_up, y_down, x_far):
+        pl.semaphore_signal(barrier, inc=1, device_id=near, device_id_type=MESH)
 
     loads = []
     for half in range(2):
@@ -107,14 +111,13 @@
     load_w = pltpu.make_async_copy(w_hbm, w, w_sem)
     for load in loads:
         load.start()
+    load_order = pltpu.make_async_copy(order_hbm, order_ref, load_sem.at[6])
+    load_owner = pltpu.make_async_copy(owner_hbm, owner_ref, load_sem.at[7])
+    load_order.start()
+    load_owner.start()
     load_q.start()
     load_w.start()
 
-    barrier = pltpu.get_barrier_semaphore()
-    for near in (z_up, z_down, x_near, core, y_up, y_down, x_far):
-        pl.semaphore_signal(barrier, inc=1, device_id=near, device_id_type=MESH)
-
-    here = order_ref[grp]
     for slot, block, half in half_blocks(z, xl, c):
         place[2 * block + half] = slot + 0 * grp
         holder[slot] = block
@@ -229,6 +232,9 @@
                 factor = jnp.exp2((old - new) * SCALE2)
                 acc[h] = acc[h] * jnp.concatenate([factor, factor], axis=1) + gained
 
+    load_order.wait()
+    load_owner.wait()
+    here = order_ref[grp]
     load_q.wait()
     lane = lax.broadcasted_iota(jnp.int32, (ROWS, HEAD), 1)
     unit = jnp.where(lane == 0, 1.0, 0.0).astype(jnp.bfloat16)
@@ -254,12 +260,10 @@
     def project(i, j):
         first = (lax.rem(y + i, 4) * 2 + (1 - xh if j else xh)) * COLS
 
-        @pl.loop(0, 4)
-        def _(n):
-            at = pl.multiple_of(first + n * 256, 256)
-            to = pl.multiple_of(n * 256, 256)
-            part[i, j, :, pl.ds(to, 256)] = jnp.dot(
-                att[...], w[:, pl.ds(at, 256)], preferred_element_type=jnp.float32).astype(jnp.bfloat16)
+        for n in range(2):
+            at = pl.multiple_of(first + n * 512, 512)
+            part[i, j, :, pl.ds(n * 512, 512)] = jnp.dot(
+                att[...], w[:, pl.ds(at, 512)], preferred_element_type=jnp.float32).astype(jnp.bfloat16)
 
     def u_rows(g):
         return pl.ds(sum(Y_ROWS[:g]), Y_ROWS[g])
@@ -379,26 +383,21 @@
         make(*which).wait_send()
 
 
-def hand_over(made, paged, out, pages):
-    out[...] = made[...]
-    pages[...] = paged[...]
-
-
 def on_device(queries, key_rows, value_rows, out_weight, block_order, page_owner):
     dma = pltpu.SemaphoreType.DMA
     vmem = pltpu.VMEM
     bf16, f32, i32 = jnp.bfloat16, jnp.float32, jnp.int32
-    smem_in = pl.BlockSpec(memory_space=pltpu.SMEM)
-    hbm_in = pl.BlockSpec(memory_space=pl.ANY)
+    hbm = pl.BlockSpec(memory_space=pltpu.HBM)
     vmem_out = pl.BlockSpec(memory_space=pltpu.VMEM)
     made = pl.pallas_call(
         kernel,
         name="attend",
-        out_shape=(jax.ShapeDtypeStruct((ROWS, COLS), bf16),
-                   jax.ShapeDtypeStruct((SLOTS, PAGE, 2 * HEAD), bf16)),
-        in_specs=[smem_in, smem_in, hbm_in, hbm_in, hbm_in, hbm_in],
+        out_shape=(vmem((ROWS, COLS), bf16), vmem((SLOTS, PAGE, 2 * HEAD), bf16)),
+        in_specs=[hbm] * 6,
         out_specs=(vmem_out, vmem_out),
         scratch_shapes=[
+            pltpu.SMEM((32,), i32),
+            pltpu.SMEM((NPAGES,), i32),
             vmem((NPAGES, PAGE, 2 * HEAD), bf16),
             vmem((ROWS, QPK * HEAD), bf16),
             vmem((QPK, ROWS, 2 * HEAD), bf16),
@@ -415,7 +414,7 @@
             pltpu.SMEM((8, 128), i32),
             pltpu.SMEM((64,), i32),
             pltpu.SMEM((64,), i32),
-            dma((6,)), dma,
+            dma((8,)), dma,
             dma((2, 11)), dma((2, 11)), dma((8,)), dma((8,)), dma((N_SET,)), dma((N_SET,)),
             dma((Y_FIRST, 2, 3)), dma((Y_FIRST, 2, 3)), dma((Y_FIRST,)), dma((Y_FIRST,)),
             dma((X_FIRST, 4)), dma((X_FIRST, 4)), dma((X_FIRST, 2, 3)), dma((X_FIRST, 2, 3)),
@@ -424,13 +423,7 @@
             collective_id=0, has_side_effects=True, vmem_limit_bytes=56 * 2**20),
     )(block_order, page_owner.reshape(NPAGES), queries,
       key_rows.reshape(PAGE, PAGE, HEAD), value_rows.reshape(PAGE, PAGE, HEAD), out_weight)
-    return pl.pallas_call(
-        hand_over,
-        name="hand_over",
-        out_shape=tuple(jax.ShapeDtypeStruct(a.shape, a.dtype) for a in made),
-        in_specs=[vmem_out, vmem_out],
-        out_specs=(vmem_out, vmem_out),
-    )(*made)
+    return made
 
 
 def solution(mesh):

time: 69.1 us -> 66.1 us (0.957)
  Pallas kernels: 68.3 us -> 63.7 us
  local copies, waits for them, and re-layouts: 0 us -> 1.59 us
    pallas_call x2 -> x1, Pallas kernels: 68.3 us -> 63.7 us  [on_device(): pl.pallas_call(kernel, name='attend', out_shape=(vmem((ROWS, COLS), bf16)...]
    unnamed x0 -> x2, local copies, waits for them, and re-layouts: none -> 1.59 us
where the time goes in v3:
time: 66.1 us; the launch traced here: 66 us
  Pallas kernels  63.7 us (96%)
  local copies, waits for them, and re-layouts  1.59 us (2%)
    pallas_call x1, Pallas kernels, on_device(): pl.pallas_call(kernel, name='attend', out_shape=(vmem((ROWS, COLS), bf16)...  63.7 us
    unnamed x2, local copies, waits for them, and re-layouts  1.59 us

profile of v3, /device:TPU:8, one launch (start us, length us, event | category | flops | bytes accessed | tf_op | source)
XLA Modules:
  0.0 66.0 jit_solution(13615140568108428118)
XLA Ops:
  0.6 63.7 %attend.1 = (bf16[256,1024]{1,0:T(8,128)(2,1)S(1)}, bf16[64,16,256]{2,1,0:T(8,128)(2,1)S(1)}) custom-call(s32[32]{0:T(128)} %order_hbm.1, s32[512]{0:T(512)} %bitcast.5, bf16[256,512]{1,0:T(8,128)(2,1)} %q_hbm.1, bf16[16,16,128]{2,1,0:T(8,128)(2,1)} %bitcast.3, bf16[16,16,128]{2,1,0:T(8,128)(2,1)} %bitcast.4, bf16[512,8192]{1,0:T(8,128)(2,1)} %w_hbm.1), custom_call_target="tpu_custom_call" | custom-call | tf_op jit(solution)/shard_map/attend/pallas_call | solution.py:392
  64.4 0.8 %copy.10 = bf16[256,1024]{1,0:T(8,128)(2,1)} copy(bf16[256,1024]{1,0:T(8,128)(2,1)S(1)} %get-tuple-element.2) | data formatting | bytes 1048576
  65.2 0.8 %copy.11 = bf16[64,16,256]{2,1,0:T(8,128)(2,1)} copy(bf16[64,16,256]{2,1,0:T(8,128)(2,1)S(1)} %get-tuple-element.3) | data formatting | bytes 1048576

commit v4 on v3

--- a/solution.py
+++ b/solution.py
@@ -22,22 +22,20 @@
 X_SET = (2, 6, 11, 14)
 N_SET = 16
 
-Y_ROWS = (48, 48, 48)
-X_ROWS = (48, 64)
+Y_ROWS = (64, 64, 32)
+X_ROWS = (48, 48)
 Y_FIRST, X_FIRST = len(Y_ROWS), len(X_ROWS)
+NEAR = sum(Y_ROWS)
 ORDER = (
-    ("p", 2, 0), ("s", "y", 0, 0, 0), ("p", 2, 1), ("s", "y", 0, 1, 0), ("s", "x", 0, 2),
-    ("p", 1, 1), ("s", "y", 0, 0, 1), ("s", "y", 1, 0, 0), ("s", "y", 1, 0, 1), ("s", "y", 2, 0, 0),
-    ("s", "y", 2, 0, 1), ("s", "x", 0, 1),
-    ("p", 3, 0), ("s", "y", 0, 1, 1), ("s", "y", 1, 1, 0), ("s", "y", 1, 1, 1), ("s", "y", 2, 1, 0),
-    ("s", "y", 2, 1, 1),
-    ("p", 3, 1), ("s", "x", 0, 3),
-    ("p", 0, 1), ("s", "x", 0, 0), ("s", "x", 1, 2), ("s", "x", 1, 1), ("s", "x", 1, 3), ("s", "x", 1, 0),
-    ("p", 1, 0), ("p", 0, 0),
-    ("ua", 0, 0), ("ua", 0, 1), ("wm", 0, 2), ("pages", 0), ("pages", 1), ("wm", 0, 1), ("pages", 2),
-    ("ua", 1, 0), ("ua", 1, 1), ("wm", 0, 3), ("pages", 3), ("ua", 2, 0), ("ua", 2, 1),
-    ("wm", 1, 2), ("wm", 1, 1), ("uc", 0), ("wa", 0, 0), ("wa", 0, 1), ("wm", 1, 3), ("uc", 1), ("uc", 2),
-    ("wa", 1, 0), ("uo", 0), ("wa", 1, 1), ("uo", 1), ("wo", 0), ("wo", 1), ("uo", 2),
+    ("p", 2, 1), ("sn", 0, 0, 0), ("sn", 0, 1, 0), ("sx", 0, 2), ("p", 1, 1), ("sn", 0, 0, 1),
+    ("sa", 0), ("sn", 1, 0, 0), ("sn", 1, 0, 1), ("sn", 2, 0, 0), ("sn", 2, 0, 1), ("sx", 0, 1), ("p", 3, 1),
+    ("sn", 0, 1, 1), ("sa", 1), ("sn", 1, 1, 0), ("sn", 1, 1, 1), ("sn", 2, 1, 0), ("sn", 2, 1, 1), ("sa", 2),
+    ("sx", 0, 3), ("p", 0, 1), ("sx", 0, 0), ("sx", 1, 2), ("sx", 1, 1), ("sx", 1, 3), ("sx", 1, 0),
+    ("p", 2, 0), ("p", 1, 0), ("p", 3, 0), ("p", 0, 0), ("forward",), ("pages", 0), ("pages", 1), ("wm", 0, 2),
+    ("na", 0, 0), ("na", 0, 1), ("pages", 2), ("pages", 3), ("wm", 0, 1), ("sum", 0), ("wm", 0, 3),
+    ("na", 1, 0), ("na", 1, 1), ("sum", 1), ("sum", 2), ("sum", 3), ("wm", 1, 2), ("na", 2, 0), ("na", 2, 1),
+    ("wa", 0, 0), ("wa", 0, 1), ("wm", 1, 1), ("nc", 0), ("wm", 1, 3), ("nc", 1), ("wa", 1, 0), ("wa", 1, 1),
+    ("nc", 2), ("wo", 0), ("no", 0), ("wo", 1), ("no", 1), ("no", 2),
 )
 
 
@@ -79,8 +77,9 @@
 
 
 def kernel(order_hbm, owner_hbm, q_hbm, k_hbm, v_hbm, w_hbm, out_ref, pages_ref,
-           order_ref, owner_ref, kv, q_raw, qx, top, acc, att, w, part, uy, ux, wx, wy, table_v, table_s, place, holder,
+           slices, gathered, own, order_ref, owner_ref, kv, q_raw, qx, top, acc, att, w, part, uy, ux, wx, wy, table_v, table_s, place, holder,
            load_sem, w_sem, z_ssem, z_rsem, x_ssem, x_rsem, d_ssem, d_rsem,
+           slice_ssem, slice_rsem, half_ssem, half_rsem, att_ssem, att_rsem,
            uy_ssem, uy_rsem, ux_ssem, ux_rsem, wx_ssem, wx_rsem, wy_ssem, wy_rsem):
     grp, tp = lax.axis_index("grp"), lax.axis_index("tp")
     z, xl, c = grp // 4, lax.rem(grp // 2, 2), lax.rem(grp, 2)
@@ -95,10 +94,11 @@
     core = at_grp(z, xl, 1 - c)
     y_up = (grp, lax.rem(y + 1, 4) * 2 + xh)
     y_down = (grp, lax.rem(y + 3, 4) * 2 + xh)
+    y_far = (grp, lax.rem(y + 2, 4) * 2 + xh)
     x_far = (grp, y * 2 + 1 - xh)
 
     barrier = pltpu.get_barrier_semaphore()
-    for near in (z_up, z_down, x_near, core, y_up, y_down, x_far):
+    for near in (z_up, z_down, x_near, core, y_up, y_down, y_far, x_far):
         pl.semaphore_signal(barrier, inc=1, device_id=near, device_id_type=MESH)
 
     loads = []
@@ -124,7 +124,7 @@
 
     for load in loads:
         load.wait()
-    pl.semaphore_wait(barrier, 7)
+    pl.semaphore_wait(barrier, 8)
 
     sent = []
 
@@ -158,6 +158,22 @@
     begin(cross, 1, 1)
     begin(plus, 1, 1)
     begin(minus, 1, 0)
+
+    ahead = (y_up, y_down, y_far)
+    steps = (1, 3, 2)
+
+    def weight_slice(n):
+        first = (lax.rem(y + steps[n], 4) * 2 + xh) * COLS
+        src = w_hbm.at[pl.ds(pl.multiple_of(256 * c, 256), 256), pl.ds(pl.multiple_of(first, COLS), COLS)]
+        return remote(src, slices.at[n, pl.ds(pl.multiple_of(256 * c, 256), 256)],
+                      slice_ssem.at[n], slice_rsem.at[n], ahead[n])
+
+    def weight_half(n):
+        half = slices.at[n, pl.ds(pl.multiple_of(256 * c, 256), 256)]
+        return remote(half, half, half_ssem.at[n], half_rsem.at[n], core)
+
+    for n in range(3):
+        begin(weight_slice, n)
 
     def z_step(r):
         plus(r, 0).wait_recv()
@@ -257,24 +273,37 @@
         att[:, HEAD * h:HEAD * (h + 1)] = (acc[h, :, :HEAD] / acc[h, :, HEAD:]).astype(jnp.bfloat16)
     load_w.wait()
 
+    def cols_of(i, j):
+        return (lax.rem(y + i, 4) * 2 + (1 - xh if j else xh)) * COLS
+
     def project(i, j):
-        first = (lax.rem(y + i, 4) * 2 + (1 - xh if j else xh)) * COLS
-
+        rows = pl.ds(0, ROWS) if j else pl.ds(NEAR, ROWS - NEAR)
         for n in range(2):
-            at = pl.multiple_of(first + n * 512, 512)
-            part[i, j, :, pl.ds(n * 512, 512)] = jnp.dot(
-                att[...], w[:, pl.ds(at, 512)], preferred_element_type=jnp.float32).astype(jnp.bfloat16)
+            at = pl.multiple_of(cols_of(i, j) + n * 512, 512)
+            part[i, j, rows, pl.ds(n * 512, 512)] = jnp.dot(
+                att[rows], w[:, pl.ds(at, 512)], preferred_element_type=jnp.float32).astype(jnp.bfloat16)
 
     def u_rows(g):
         return pl.ds(sum(Y_ROWS[:g]), Y_ROWS[g])
 
     def w_rows(g):
-        return pl.ds(sum(Y_ROWS) + sum(X_ROWS[:g]), X_ROWS[g])
+        return pl.ds(NEAR + sum(X_ROWS[:g]), X_ROWS[g])
+
+    def att_rows(n):
+        return remote(att.at[pl.ds(0, NEAR)], gathered.at[n], att_ssem.at[n], att_rsem.at[n], ahead[n])
+
+    def along_y(way, n, j, rows, to, ssem, rsem):
+        i = (2, 1, 1)[n] if way == 0 else (2, 3, 3)[n]
+        left = (0, 1, 0)[n] if way == 0 else (1, 0, 1)[n]
+        return remote(part.at[i, j, rows, pl.ds(512 * left, 512)], to, ssem, rsem, (y_up, y_down)[way])
 
     def u_near(g, way, n):
-        i, j = ((2, 0), (1, 1), (1, 0))[n] if way == 0 else ((2, 1), (3, 0), (3, 1))[n]
-        return remote(part.at[i, j, u_rows(g)], uy.at[g, way, n, pl.ds(0, Y_ROWS[g])],
-                      uy_ssem.at[g, way, n], uy_rsem.at[g, way, n], (y_up, y_down)[way])
+        return along_y(way, n, 1, u_rows(g), uy.at[g, way, n, pl.ds(0, Y_ROWS[g])],
+                       uy_ssem.at[g, way, n], uy_rsem.at[g, way, n])
+
+    def w_near(g, way, n):
+        return along_y(way, n, 0, w_rows(g), wy.at[g, way, n, pl.ds(0, X_ROWS[g])],
+                       wy_ssem.at[g, way, n], wy_rsem.at[g, way, n])
 
     def u_far(g):
         return remote(part.at[0, 1, u_rows(g)], ux.at[g, pl.ds(0, Y_ROWS[g])], ux_ssem.at[g], ux_rsem.at[g], x_far)
@@ -283,36 +312,49 @@
         return remote(part.at[i, 1, w_rows(g)], wx.at[g, i, pl.ds(0, X_ROWS[g])],
                       wx_ssem.at[g, i], wx_rsem.at[g, i], x_far)
 
-    def w_near(g, way, n):
-        i = (2, 1, 1)[n] if way == 0 else (2, 3, 3)[n]
-        left = (0, 1, 0)[n] if way == 0 else (1, 0, 1)[n]
-        return remote(part.at[i, 0, w_rows(g), pl.ds(512 * left, 512)], wy.at[g, way, n, pl.ds(0, X_ROWS[g])],
-                      wy_ssem.at[g, way, n], wy_rsem.at[g, way, n], (y_up, y_down)[way])
-
     def wide(a):
         return a.astype(jnp.float32)
 
-    def u_add(g, way):
-        i, j = ((1, 0), (3, 1))[way]
-        u_near(g, way, 0).wait_recv()
-        came = uy[g, way, 0, :Y_ROWS[g]]
-        part[i, j, u_rows(g)] = (wide(part[i, j, u_rows(g)]) + wide(came)).astype(jnp.bfloat16)
-        begin(u_near, g, way, 2)
-
-    def u_total(g, j):
-        size = Y_ROWS[g]
-        return wide(part[0, j, u_rows(g)]) + wide(uy[g, 0, 2 - j, :size]) + wide(uy[g, 1, 1 + j, :size])
-
-    def u_cross(g):
+    def add_half(near, j, rows, came, g, way):
+        i, cols = (1, 3)[way], pl.ds(512 * way, 512)
+        near(g, way, 0).wait_recv()
+        part[i, j, rows, cols] = (wide(part[i, j, rows, cols]) + wide(came())).astype(jnp.bfloat16)
+        begin(near, g, way, 2)
+
+    def both_ways(near, g):
         for way in (0, 1):
             for n in (1, 2):
-                u_near(g, way, n).wait_recv()
-        part[0, 1, u_rows(g)] = u_total(g, 1).astype(jnp.bfloat16)
+                near(g, way, n).wait_recv()
+
+    def came_along_y(buf, g, size):
+        return jnp.concatenate([wide(buf[g, 0, 2 - left, :size]) + wide(buf[g, 1, 1 + left, :size])
+                                for left in (0, 1)], axis=1)
+
+    def u_add(g, way):
+        add_half(u_near, 1, u_rows(g), lambda: uy[g, way, 0, :Y_ROWS[g]], g, way)
+
+    def u_cross(g):
+        both_ways(u_near, g)
+        part[0, 1, u_rows(g)] = (wide(part[0, 1, u_rows(g)]) + came_along_y(uy, g, Y_ROWS[g])).astype(jnp.bfloat16)
         begin(u_far, g)
 
     def u_out(g):
         u_far(g).wait_recv()
-        out_ref[u_rows(g)] = (u_total(g, 0) + wide(ux[g, :Y_ROWS[g]])).astype(jnp.bfloat16)
+        out_ref[u_rows(g)] = (own[u_rows(g)] + wide(ux[g, :Y_ROWS[g]])).astype(jnp.bfloat16)
+
+    def forward():
+        for n in range(3):
+            weight_slice(n).wait_recv()
+            begin(weight_half, n)
+
+    def own_sum(n):
+        if n == 0:
+            at = pl.multiple_of(cols_of(0, 0), COLS)
+            own[...] = jnp.dot(att[pl.ds(0, NEAR)], w[:, pl.ds(at, COLS)], preferred_element_type=jnp.float32)
+        else:
+            att_rows(n - 1).wait_recv()
+            weight_half(n - 1).wait_recv()
+            own[...] += jnp.dot(gathered[n - 1], slices[n - 1], preferred_element_type=jnp.float32)
 
     def w_mid(g, i):
         at = w_rows(g)
@@ -325,22 +367,14 @@
             begin(w_near, g, (1 if i == 3 else 0), 1)
 
     def w_add(g, way):
-        at, cols = w_rows(g), pl.ds(512 * way, 512)
-        i = (1, 3)[way]
-        w_near(g, way, 0).wait_recv()
-        came = wy[g, way, 0, :X_ROWS[g]]
-        part[i, 0, at, cols] = (wide(part[i, 0, at, cols]) + wide(came)).astype(jnp.bfloat16)
-        begin(w_near, g, way, 2)
+        add_half(w_near, 0, w_rows(g), lambda: wy[g, way, 0, :X_ROWS[g]], g, way)
 
     def w_out(g):
         at, size = w_rows(g), X_ROWS[g]
         w_far(g, 0).wait_recv()
-        for way in (0, 1):
-            for n in (1, 2):
-                w_near(g, way, n).wait_recv()
-        total = wide(part[0, 0, at]) + wide(wx[g, 0, :size])
-        came = [wide(wy[g, 0, 2 - left, :size]) + wide(wy[g, 1, 1 + left, :size]) for left in (0, 1)]
-        out_ref[at] = (total + jnp.concatenate(came, axis=1)).astype(jnp.bfloat16)
+        both_ways(w_near, g)
+        total = wide(part[0, 0, at]) + wide(wx[g, 0, :size]) + came_along_y(wy, g, size)
+        out_ref[at] = total.astype(jnp.bfloat16)
 
     def find_pages():
         lanes = lax.broadcasted_iota(jnp.int32, (8, 128), 1)
@@ -370,14 +404,15 @@
     for step, *which in ORDER:
         if step == "p":
             project(*which)
-        elif step == "s":
-            begin(u_near if which[0] == "y" else w_far, *which[1:])
+        elif step in ("sa", "sn", "sx"):
+            begin({"sa": att_rows, "sn": u_near, "sx": w_far}[step], *which)
         elif step == "pages":
             if which[0] == 0:
                 owned = find_pages()
             hand_pages(which[0] * (SLOTS // 4), owned)
         else:
-            {"ua": u_add, "uc": u_cross, "uo": u_out, "wm": w_mid, "wa": w_add, "wo": w_out}[step](*which)
+            {"na": u_add, "nc": u_cross, "no": u_out, "wm": w_mid, "wa": w_add, "wo": w_out,
+             "forward": forward, "sum": own_sum}[step](*which)
 
     for make, which in sent:
         make(*which).wait_send()
@@ -396,6 +431,9 @@
         in_specs=[hbm] * 6,
         out_specs=(vmem_out, vmem_out),
         scratch_shapes=[
+            vmem((3, QPK * HEAD, COLS), bf16),
+            vmem((3, NEAR, QPK * HEAD), bf16),
+            vmem((NEAR, COLS), f32),
             pltpu.SMEM((32,), i32),
             pltpu.SMEM((NPAGES,), i32),
             vmem((NPAGES, PAGE, 2 * HEAD), bf16),
@@ -406,7 +444,7 @@
             vmem((ROWS, QPK * HEAD), bf16),
             vmem((QPK * HEAD, 8 * COLS), bf16),
             vmem((4, 2, ROWS, COLS), bf16),
-            vmem((Y_FIRST, 2, 3, max(Y_ROWS), COLS), bf16),
+            vmem((Y_FIRST, 2, 3, max(Y_ROWS), COLS // 2), bf16),
             vmem((Y_FIRST, max(Y_ROWS), COLS), bf16),
             vmem((X_FIRST, 4, max(X_ROWS), COLS), bf16),
             vmem((X_FIRST, 2, 3, max(X_ROWS), COLS // 2), bf16),
@@ -416,6 +454,7 @@
             pltpu.SMEM((64,), i32),
             dma((8,)), dma,
             dma((2, 11)), dma((2, 11)), dma((8,)), dma((8,)), dma((N_SET,)), dma((N_SET,)),
+            dma((3,)), dma((3,)), dma((3,)), dma((3,)), dma((3,)), dma((3,)),
             dma((Y_FIRST, 2, 3)), dma((Y_FIRST, 2, 3)), dma((Y_FIRST,)), dma((Y_FIRST,)),
             dma((X_FIRST, 4)), dma((X_FIRST, 4)), dma((X_FIRST, 2, 3)), dma((X_FIRST, 2, 3)),
         ],

time: 66.1 us -> 64.6 us (0.977)
  Pallas kernels: 63.7 us -> 62.2 us
    pallas_call x1, Pallas kernels: 63.7 us -> 62.2 us  [on_device(): pl.pallas_call(kernel, name='attend', out_shape=(vmem((ROWS, COLS), bf16)...]
where the time goes in v4:
time: 64.6 us; the launch traced here: 64.4 us
  Pallas kernels  62.2 us (96%)
  local copies, waits for them, and re-layouts  1.59 us (2%)
    pallas_call x1, Pallas kernels, on_device(): pl.pallas_call(kernel, name='attend', out_shape=(vmem((ROWS, COLS), bf16)...  62.2 us
    unnamed x2, local copies, waits for them, and re-layouts  1.59 us

profile of v4, /device:TPU:8, one launch (start us, length us, event | category | flops | bytes accessed | tf_op | source)
XLA Modules:
  0.0 64.4 jit_solution(5522627159967434734)
XLA Ops:
  0.6 62.2 %attend.1 = (bf16[256,1024]{1,0:T(8,128)(2,1)S(1)}, bf16[64,16,256]{2,1,0:T(8,128)(2,1)S(1)}) custom-call(s32[32]{0:T(128)} %order_hbm.1, s32[512]{0:T(512)} %bitcast.5, bf16[256,512]{1,0:T(8,128)(2,1)} %q_hbm.1, bf16[16,16,128]{2,1,0:T(8,128)(2,1)} %bitcast.3, bf16[16,16,128]{2,1,0:T(8,128)(2,1)} %bitcast.4, bf16[512,8192]{1,0:T(8,128)(2,1)} %w_hbm.1), custom_call_target="tpu_custom_call" | custom-call | tf_op jit(solution)/shard_map/attend/pallas_call | solution.py:427
  62.8 0.8 %copy.10 = bf16[256,1024]{1,0:T(8,128)(2,1)} copy(bf16[256,1024]{1,0:T(8,128)(2,1)S(1)} %get-tuple-element.2) | data formatting | bytes 1048576
  63.6 0.8 %copy.11 = bf16[64,16,256]{2,1,0:T(8,128)(2,1)} copy(bf16[64,16,256]{2,1,0:T(8,128)(2,1)S(1)} %get-tuple-element.3) | data formatting | bytes 1048576

commit v5 on v4

--- a/solution.py
+++ b/solution.py
@@ -29,12 +29,12 @@
 ORDER = (
     ("p", 2, 1), ("sn", 0, 0, 0), ("sn", 0, 1, 0), ("sx", 0, 2), ("p", 1, 1), ("sn", 0, 0, 1),
     ("sa", 0), ("sn", 1, 0, 0), ("sn", 1, 0, 1), ("sn", 2, 0, 0), ("sn", 2, 0, 1), ("sx", 0, 1), ("p", 3, 1),
-    ("sn", 0, 1, 1), ("sa", 1), ("sn", 1, 1, 0), ("sn", 1, 1, 1), ("sn", 2, 1, 0), ("sn", 2, 1, 1), ("sa", 2),
+    ("sn", 0, 1, 1), ("sa", 1), ("sn", 1, 1, 0), ("sn", 1, 1, 1), ("sn", 2, 1, 0), ("sn", 2, 1, 1),
     ("sx", 0, 3), ("p", 0, 1), ("sx", 0, 0), ("sx", 1, 2), ("sx", 1, 1), ("sx", 1, 3), ("sx", 1, 0),
     ("p", 2, 0), ("p", 1, 0), ("p", 3, 0), ("p", 0, 0), ("forward",), ("pages", 0), ("pages", 1), ("wm", 0, 2),
     ("na", 0, 0), ("na", 0, 1), ("pages", 2), ("pages", 3), ("wm", 0, 1), ("sum", 0), ("wm", 0, 3),
-    ("na", 1, 0), ("na", 1, 1), ("sum", 1), ("sum", 2), ("sum", 3), ("wm", 1, 2), ("na", 2, 0), ("na", 2, 1),
-    ("wa", 0, 0), ("wa", 0, 1), ("wm", 1, 1), ("nc", 0), ("wm", 1, 3), ("nc", 1), ("wa", 1, 0), ("wa", 1, 1),
+    ("relay", 0), ("relay", 1), ("na", 1, 0), ("na", 1, 1), ("sum", 1), ("sum", 2), ("wm", 1, 2), ("na", 2, 0), ("na", 2, 1),
+    ("wa", 0, 0), ("wa", 0, 1), ("wm", 1, 1), ("nc", 0), ("sum", 3), ("wm", 1, 3), ("nc", 1), ("wa", 1, 0), ("wa", 1, 1),
     ("nc", 2), ("wo", 0), ("no", 0), ("wo", 1), ("no", 1), ("no", 2),
 )
 
@@ -292,6 +292,15 @@
     def att_rows(n):
         return remote(att.at[pl.ds(0, NEAR)], gathered.at[n], att_ssem.at[n], att_rsem.at[n], ahead[n])
 
+    def att_relay(way):
+        half = pl.ds(NEAR // 2 * way, NEAR // 2)
+        return remote(gathered.at[way, half], gathered.at[2, half], att_ssem.at[2 + way], att_rsem.at[2 + way],
+                      ahead[way])
+
+    def relay(way):
+        att_rows(way).wait_recv()
+        begin(att_relay, way)
+
     def along_y(way, n, j, rows, to, ssem, rsem):
         i = (2, 1, 1)[n] if way == 0 else (2, 3, 3)[n]
         left = (0, 1, 0)[n] if way == 0 else (1, 0, 1)[n]
@@ -352,7 +361,9 @@
             at = pl.multiple_of(cols_of(0, 0), COLS)
             own[...] = jnp.dot(att[pl.ds(0, NEAR)], w[:, pl.ds(at, COLS)], preferred_element_type=jnp.float32)
         else:
-            att_rows(n - 1).wait_recv()
+            if n == 3:
+                att_relay(0).wait_recv()
+                att_relay(1).wait_recv()
             weight_half(n - 1).wait_recv()
             own[...] += jnp.dot(gathered[n - 1], slices[n - 1], preferred_element_type=jnp.float32)
 
@@ -412,7 +423,7 @@
             hand_pages(which[0] * (SLOTS // 4), owned)
         else:
             {"na": u_add, "nc": u_cross, "no": u_out, "wm": w_mid, "wa": w_add, "wo": w_out,
-             "forward": forward, "sum": own_sum}[step](*which)
+             "forward": forward, "relay": relay, "sum": own_sum}[step](*which)
 
     for make, which in sent:
         make(*which).wait_send()
@@ -454,7 +465,7 @@
             pltpu.SMEM((64,), i32),
             dma((8,)), dma,
             dma((2, 11)), dma((2, 11)), dma((8,)), dma((8,)), dma((N_SET,)), dma((N_SET,)),
-            dma((3,)), dma((3,)), dma((3,)), dma((3,)), dma((3,)), dma((3,)),
+            dma((3,)), dma((3,)), dma((3,)), dma((3,)), dma((4,)), dma((4,)),
             dma((Y_FIRST, 2, 3)), dma((Y_FIRST, 2, 3)), dma((Y_FIRST,)), dma((Y_FIRST,)),
             dma((X_FIRST, 4)), dma((X_FIRST, 4)), dma((X_FIRST, 2, 3)), dma((X_FIRST, 2, 3)),
         ],

time: 64.6 us -> 62.9 us (0.974)
  Pallas kernels: 62.2 us -> 60.4 us
    pallas_call x1, Pallas kernels: 62.2 us -> 60.4 us  [on_device(): pl.pallas_call(kernel, name='attend', out_shape=(vmem((ROWS, COLS), bf16)...]
where the time goes in v5:
time: 62.9 us; the launch traced here: 62.7 us
  Pallas kernels  60.4 us (96%)
  local copies, waits for them, and re-layouts  1.59 us (3%)
  between operations  0.64 us (1%)
    pallas_call x1, Pallas kernels, on_device(): pl.pallas_call(kernel, name='attend', out_shape=(vmem((ROWS, COLS), bf16)...  60.4 us
    unnamed x2, local copies, waits for them, and re-layouts  1.59 us

profile of v5, /device:TPU:8, one launch (start us, length us, event | category | flops | bytes accessed | tf_op | source)
XLA Modules:
  0.0 62.7 jit_solution(11835086408643465176)
XLA Ops:
  0.6 60.4 %attend.1 = (bf16[256,1024]{1,0:T(8,128)(2,1)S(1)}, bf16[64,16,256]{2,1,0:T(8,128)(2,1)S(1)}) custom-call(s32[32]{0:T(128)} %order_hbm.1, s32[512]{0:T(512)} %bitcast.5, bf16[256,512]{1,0:T(8,128)(2,1)} %q_hbm.1, bf16[16,16,128]{2,1,0:T(8,128)(2,1)} %bitcast.3, bf16[16,16,128]{2,1,0:T(8,128)(2,1)} %bitcast.4, bf16[512,8192]{1,0:T(8,128)(2,1)} %w_hbm.1), custom_call_target="tpu_custom_call" | custom-call | tf_op jit(solution)/shard_map/attend/pallas_call | solution.py:438
  61.1 0.8 %copy.10 = bf16[256,1024]{1,0:T(8,128)(2,1)} copy(bf16[256,1024]{1,0:T(8,128)(2,1)S(1)} %get-tuple-element.2) | data formatting | bytes 1048576
  61.9 0.8 %copy.11 = bf16[64,16,256]{2,1,0:T(8,128)(2,1)} copy(bf16[64,16,256]{2,1,0:T(8,128)(2,1)S(1)} %get-tuple-element.3) | data formatting | bytes 1048576

commit v6 on v5

--- a/solution.py
+++ b/solution.py
@@ -27,9 +27,10 @@
 Y_FIRST, X_FIRST = len(Y_ROWS), len(X_ROWS)
 NEAR = sum(Y_ROWS)
 ORDER = (
+    ("sa", 0), ("sa", 1),
     ("p", 2, 1), ("sn", 0, 0, 0), ("sn", 0, 1, 0), ("sx", 0, 2), ("p", 1, 1), ("sn", 0, 0, 1),
-    ("sa", 0), ("sn", 1, 0, 0), ("sn", 1, 0, 1), ("sn", 2, 0, 0), ("sn", 2, 0, 1), ("sx", 0, 1), ("p", 3, 1),
-    ("sn", 0, 1, 1), ("sa", 1), ("sn", 1, 1, 0), ("sn", 1, 1, 1), ("sn", 2, 1, 0), ("sn", 2, 1, 1),
+    ("sn", 1, 0, 0), ("sn", 1, 0, 1), ("sn", 2, 0, 0), ("sn", 2, 0, 1), ("sx", 0, 1), ("p", 3, 1),
+    ("sn", 0, 1, 1), ("sn", 1, 1, 0), ("sn", 1, 1, 1), ("sn", 2, 1, 0), ("sn", 2, 1, 1),
     ("sx", 0, 3), ("p", 0, 1), ("sx", 0, 0), ("sx", 1, 2), ("sx", 1, 1), ("sx", 1, 3), ("sx", 1, 0),
     ("p", 2, 0), ("p", 1, 0), ("p", 3, 0), ("p", 0, 0), ("forward",), ("pages", 0), ("pages", 1), ("wm", 0, 2),
     ("na", 0, 0), ("na", 0, 1), ("pages", 2), ("pages", 3), ("wm", 0, 1), ("sum", 0), ("wm", 0, 3),

time: 62.9 us -> 62.7 us (level)
  no operation moved by 1% of the time
where the time goes in v6:
time: 62.7 us; the launch traced here: 62.3 us
  Pallas kernels  60.1 us (96%)
  local copies, waits for them, and re-layouts  1.59 us (3%)
  between operations  0.64 us (1%)
    pallas_call x1, Pallas kernels, on_device(): pl.pallas_call(kernel, name='attend', out_shape=(vmem((ROWS, COLS), bf16)...  60.1 us
    unnamed x2, local copies, waits for them, and re-layouts  1.59 us

profile of v6, /device:TPU:8, one launch (start us, length us, event | category | flops | bytes accessed | tf_op | source)
XLA Modules:
  0.0 62.3 jit_solution(10129657633266805954)
XLA Ops:
  0.6 60.1 %attend.1 = (bf16[256,1024]{1,0:T(8,128)(2,1)S(1)}, bf16[64,16,256]{2,1,0:T(8,128)(2,1)S(1)}) custom-call(s32[32]{0:T(128)} %order_hbm.1, s32[512]{0:T(512)} %bitcast.5, bf16[256,512]{1,0:T(8,128)(2,1)} %q_hbm.1, bf16[16,16,128]{2,1,0:T(8,128)(2,1)} %bitcast.3, bf16[16,16,128]{2,1,0:T(8,128)(2,1)} %bitcast.4, bf16[512,8192]{1,0:T(8,128)(2,1)} %w_hbm.1), custom_call_target="tpu_custom_call" | custom-call | tf_op jit(solution)/shard_map/attend/pallas_call | solution.py:439
  60.7 0.8 %copy.10 = bf16[256,1024]{1,0:T(8,128)(2,1)} copy(bf16[256,1024]{1,0:T(8,128)(2,1)S(1)} %get-tuple-element.2) | data formatting | bytes 1048576
  61.5 0.8 %copy.11 = bf16[64,16,256]{2,1,0:T(8,128)(2,1)} copy(bf16[64,16,256]{2,1,0:T(8,128)(2,1)S(1)} %get-tuple-element.3) | data formatting | bytes 1048576

commit v7 on v6

--- a/solution.py
+++ b/solution.py
@@ -33,8 +33,8 @@
     ("sn", 0, 1, 1), ("sn", 1, 1, 0), ("sn", 1, 1, 1), ("sn", 2, 1, 0), ("sn", 2, 1, 1),
     ("sx", 0, 3), ("p", 0, 1), ("sx", 0, 0), ("sx", 1, 2), ("sx", 1, 1), ("sx", 1, 3), ("sx", 1, 0),
     ("p", 2, 0), ("p", 1, 0), ("p", 3, 0), ("p", 0, 0), ("forward",), ("pages", 0), ("pages", 1), ("wm", 0, 2),
-    ("na", 0, 0), ("na", 0, 1), ("pages", 2), ("pages", 3), ("wm", 0, 1), ("sum", 0), ("wm", 0, 3),
-    ("relay", 0), ("relay", 1), ("na", 1, 0), ("na", 1, 1), ("sum", 1), ("sum", 2), ("wm", 1, 2), ("na", 2, 0), ("na", 2, 1),
+    ("relay", 0), ("relay", 1), ("na", 0, 0), ("na", 0, 1), ("pages", 2), ("pages", 3), ("wm", 0, 1), ("sum", 0), ("wm", 0, 3),
+    ("na", 1, 0), ("na", 1, 1), ("sum", 1), ("sum", 2), ("wm", 1, 2), ("na", 2, 0), ("na", 2, 1),
     ("wa", 0, 0), ("wa", 0, 1), ("wm", 1, 1), ("nc", 0), ("sum", 3), ("wm", 1, 3), ("nc", 1), ("wa", 1, 0), ("wa", 1, 1),
     ("nc", 2), ("wo", 0), ("no", 0), ("wo", 1), ("no", 1), ("no", 2),
 )

time: 62.7 us -> 62.4 us (level)
  no operation moved by 1% of the time
where the time goes in v7:
time: 62.4 us; the launch traced here: 62.3 us
  Pallas kernels  60.1 us (96%)
  local copies, waits for them, and re-layouts  1.59 us (3%)
  between operations  0.64 us (1%)
    pallas_call x1, Pallas kernels, on_device(): pl.pallas_call(kernel, name='attend', out_shape=(vmem((ROWS, COLS), bf16)...  60.1 us
    unnamed x2, local copies, waits for them, and re-layouts  1.59 us

profile of v7, /device:TPU:8, one launch (start us, length us, event | category | flops | bytes accessed | tf_op | source)
XLA Modules:
  0.0 62.3 jit_solution(18137008163129942455)
XLA Ops:
  0.6 60.1 %attend.1 = (bf16[256,1024]{1,0:T(8,128)(2,1)S(1)}, bf16[64,16,256]{2,1,0:T(8,128)(2,1)S(1)}) custom-call(s32[32]{0:T(128)} %order_hbm.1, s32[512]{0:T(512)} %bitcast.5, bf16[256,512]{1,0:T(8,128)(2,1)} %q_hbm.1, bf16[16,16,128]{2,1,0:T(8,128)(2,1)} %bitcast.3, bf16[16,16,128]{2,1,0:T(8,128)(2,1)} %bitcast.4, bf16[512,8192]{1,0:T(8,128)(2,1)} %w_hbm.1), custom_call_target="tpu_custom_call" | custom-call | tf_op jit(solution)/shard_map/attend/pallas_call | solution.py:439
  60.7 0.8 %copy.10 = bf16[256,1024]{1,0:T(8,128)(2,1)} copy(bf16[256,1024]{1,0:T(8,128)(2,1)S(1)} %get-tuple-element.2) | data formatting | bytes 1048576
  61.5 0.8 %copy.11 = bf16[64,16,256]{2,1,0:T(8,128)(2,1)} copy(bf16[64,16,256]{2,1,0:T(8,128)(2,1)S(1)} %get-tuple-element.3) | data formatting | bytes 1048576
